TPU v7x, 128 devices: a whole 4x4x4 slice. The times are simulated.
128 devices in a mesh: leaf: 128 (over x, z, y, core).
Axes of the slice: x: 4, y: 4, z: 4, core: 2. Of those that a mesh axis runs over, the one named last changes fastest.
Arguments:
- points: bfloat16 [64, 524288], P(None, 'leaf'), may hold values from -6 to 6
- coords: float32 [3, 524288], P(None, 'leaf'), may hold values from 0 to 9
- leaf_order: int32 [524288], P('leaf'), may hold values from 0 to 524287, as said below
- leaf_basis: bfloat16 [2048, 64, 256], P('leaf'), may hold values from -0.375 to 0.375
- transfer: bfloat16 [2048, 64, 64], P('leaf'), may hold values from -0.25 to 0.25
- far_coupling: bfloat16 [16384, 64, 64], P('leaf'), may hold values from -0.75 to 0.75
- far_target: int32 [16384], P('leaf'), may hold values from 0 to 15
- far_source: int32 [16384], P('leaf'), may hold values from 0 to 2047, as said below
- far_live: int32 [16384], P('leaf'), may hold values 0 or 1
- top_coupling: bfloat16 [4096, 64, 64], P('leaf'), may hold values from -0.75 to 0.75
- top_target: int32 [4096], P('leaf'), may hold values from 0 to 1
- top_source: int32 [4096], P('leaf'), may hold values from 0 to 255, as said below
- top_live: int32 [4096], P('leaf'), may hold values 0 or 1
- near_source: int32 [2048, 12], P('leaf'), may hold values from 0 to 2047, as said below
- near_count: int32 [2048], P('leaf'), may hold values from 2 to 12, as said below
Outputs:
- product: bfloat16 [64, 524288], P(None, 'leaf')
Inputs may be any that keep to these rules, and one draw needn't show every extreme that they name: `leaf_order`: within each block of 4096 positions, a permutation of the input indices of that same block. `far_source`: among the 128 slots of one device, at most 2 name leaves of any one device, and in each device's slots some device is named exactly 2 times. `top_source`: among the 32 slots of one device, at most 2 name parents of any one device, and in each device's slots some device is named exactly 2 times. near_source[t, 0] = t, and every entry of row t lies within 4 of t. `near_count`: some leaf has 12.
All inputs are finite; a program needn't handle non-finite values. No bound on the sum of `far_live` or of `top_live` on one device may be relied on, other than what follows from the above.
Results may differ from a plain program's by a relative error of at most 0.0045.
The roundings to bfloat16 on the way count: a program that leaves them out, or rounds other values in their place, can miss the bound.
Values may be sent and summed in bfloat16 or wider, within the bound.
No kernel may reach another device: no remote copies, remote signals or barrier semaphores. Data moves between devices by JAX's collectives and lax.ppermute only.
A program may use at most 64 MiB of HBM per device.

v0:
```python
import functools

import jax
import jax.numpy as jnp
from jax import lax
from jax.experimental import pallas as pl
from jax.experimental.pallas import tpu as pltpu
from jax.sharding import PartitionSpec as P

delta_square = 0.0025
AXIS = "leaf"
ROWS = 16
GROUP = 4
WIDE = 8
CHUNK = 32
REPEAT = 16
UNROLL = 32
MOST_VMEM = 60 * 1024 * 1024
SOME_VMEM = 40 * 1024 * 1024
SEND_VMEM = SOME_VMEM
LAST_VMEM = 61 * 1024 * 1024
F32 = jnp.float32
BF16 = jnp.bfloat16

NT = (((1,), (1,)), ((), ()))
TN = (((0,), (0,)), ((), ()))


def mm(a, b, dims=(((1,), (0,)), ((), ()))):
    return lax.dot_general(a, b, dims, preferred_element_type=F32)


def log2(n):
    return n.bit_length() - 1


def three_parts(v):
    hi = v.astype(BF16).astype(F32)
    mid = (v - hi).astype(BF16).astype(F32)
    return hi, mid, (v - hi) - mid


def order_rows(order_ref, base, t, count=1):
    rows = [order_ref[pl.ds(2 * t + h, 1), :] for h in range(2 * count)]
    return jnp.concatenate(rows, axis=1) - base


def fetch(pairs, sems):
    copies = [pltpu.make_async_copy(src, dst, sems.at[i]) for i, (src, dst) in enumerate(pairs)]
    for copy in copies:
        copy.start()
    return copies


def tree_kernel(
    base_ref, points_hbm, coords_hbm, order_hbm, basis_hbm, transfer_hbm, far_ref, top_ref,
    tree_hbm, head_hbm, tail_hbm, table_hbm, first_hbm,
    points_ref, coords_ref, order_ref, basis_ref, transfer_ref, stacked, parts, extra, sems,
    tree_ref, table_ref, first_ref, upward, out_sems, first_sem,
):
    copies = fetch(
        [
            (order_hbm, order_ref), (coords_hbm, coords_ref), (points_hbm, points_ref),
            (basis_hbm, basis_ref), (transfer_hbm, transfer_ref),
        ],
        sems,
    )
    leaves, rank_k, pts = basis_ref.shape
    vectors = points_ref.shape[0]
    height = vectors + ROWS
    reach = head_hbm.shape[0]
    base = base_ref[0]
    parts[...] = jnp.zeros(parts.shape, F32)
    for copy in copies[:3]:
        copy.wait()
    hi, mid, lo = three_parts(coords_ref[...])
    parts[0:3, :] = hi
    parts[3:6, :] = mid
    parts[6:9, :] = lo
    for q in range(leaves):
        stacked[q * height : q * height + vectors, :] = points_ref[:, q * pts : (q + 1) * pts]
        stacked[q * height + vectors : (q + 1) * height, :] = parts[
            :, q * pts : (q + 1) * pts
        ].astype(BF16)
    row_id = lax.broadcasted_iota(jnp.int32, (pts, WIDE * pts), 0)
    for copy in copies[3:]:
        copy.wait()

    def gather(g, carry):
        local = order_rows(order_ref, base, g * WIDE, WIDE)
        low = local & (pts - 1)
        high = local >> log2(pts)
        onehot = jnp.where(row_id == low, 1.0, 0.0).astype(BF16)
        spread = mm(stacked[...], onehot)
        both = jnp.zeros((height, WIDE * pts), F32)
        for q in range(leaves):
            both = jnp.where(high == q, spread[q * height : (q + 1) * height, :], both)
        both = both.astype(BF16)
        for i in range(WIDE):
            t = g * WIDE + i
            found = both[:, i * pts : (i + 1) * pts]
            tree_ref[t] = found
            twice = jnp.concatenate([found[:vectors], found[:vectors]], axis=0)
            coeff = mm(basis_ref[t], twice, NT)
            left = lax.broadcasted_iota(jnp.int32, coeff.shape, 1) < vectors
            table_ref[0, t] = jnp.where(left, coeff, 0.0).astype(BF16)
            table_ref[1, t] = jnp.where(left, 0.0, coeff).astype(BF16)
            coeff = coeff.astype(BF16)
        return carry

    lax.fori_loop(0, leaves // WIDE, gather, 0)
    out_copies = fetch(
        [
            (table_ref, table_hbm), (tree_ref, tree_hbm), (tree_ref.at[0:reach], head_hbm),
            (tree_ref.at[leaves - reach : leaves], tail_hbm),
        ],
        out_sems,
    )
    half = rank_k // 2
    parents = leaves // 8
    extra[...] = jnp.zeros(extra.shape, F32)
    extra[0:1, :] = (far_ref[...] >> log2(leaves)).astype(F32)
    extra[1:2, :] = (far_ref[...] & (leaves - 1)).astype(F32)
    tops = top_ref.shape[1]
    extra[2:3, 0:tops] = (top_ref[...] >> log2(parents)).astype(F32)
    extra[3:4, 0:tops] = (top_ref[...] & (parents - 1)).astype(F32)
    packed = []
    for q in range(parents):
        total = jnp.zeros((rank_k, 2 * vectors), F32)
        for c in range(8 * q, 8 * q + 8):
            total = total + mm(transfer_ref[c], table_ref[0, c] + table_ref[1, c])
        left = lax.broadcasted_iota(jnp.int32, (half, 2 * vectors), 1) < vectors
        block = jnp.where(left, total[:half], total[half:])
        packed.append(jnp.concatenate([block, extra[...]], axis=0).astype(BF16))

    part = first_ref.shape[0]
    for i in range(part // parents):
        for q in range(parents):
            first_ref[parents * i + q] = packed[q]
    peers = first_hbm.shape[0]
    for i in range(peers // part):
        pltpu.make_async_copy(
            first_ref, first_hbm.at[i * part : (i + 1) * part], first_sem.at[i]
        ).start()
    for i in range(peers // part):
        pltpu.make_async_copy(
            first_ref, first_hbm.at[i * part : (i + 1) * part], first_sem.at[i]
        ).wait()
    for copy in out_copies:
        copy.wait()


def send_kernel(
    me_ref, first_ref, table_hbm, out_hbm, table_ref, out_ref, picks, picks_s, sem, table_sem, sems
):
    table_copy = pltpu.make_async_copy(table_hbm, table_ref, table_sem)
    table_copy.start()
    leaves, rank_k = table_ref.shape[1:3]
    peers, tall, lanes = first_ref.shape
    half = rank_k // 2
    asked = first_ref[:, half:tall].astype(F32)
    owner, local = asked[:, 0], asked[:, 1]
    place = lax.broadcasted_iota(jnp.int32, owner.shape, 1).astype(F32)
    mine = owner == me_ref[0].astype(F32)
    key = place * leaves + local
    first = jnp.min(jnp.where(mine, key, float(lanes * leaves)), axis=1, keepdims=True)
    last = jnp.max(jnp.where(mine, key, -1.0), axis=1, keepdims=True)
    column = lax.broadcasted_iota(jnp.int32, owner.shape, 1)
    both = jnp.where(column == 0, first, jnp.where(column == 1, last, 0.0)).T[:8]
    picks[...] = both.astype(jnp.int32) & (leaves - 1)
    copy = pltpu.make_async_copy(picks, picks_s, sem)
    copy.start()
    copy.wait()

    def fill(d, carry):
        out_ref[d] = table_ref[0, picks_s[0, d]] + table_ref[1, picks_s[1, d]]
        return carry

    table_copy.wait()
    pieces = sems.shape[0]
    part = peers // pieces
    copies = []
    for i in range(pieces):
        span = slice(i * part, (i + 1) * part)
        lax.fori_loop(i * part, (i + 1) * part, fill, 0, unroll=8)
        copies.append(pltpu.make_async_copy(out_ref.at[span], out_hbm.at[span], sems.at[i]))
        copies[-1].start()
    for copy in copies:
        copy.wait()


def gift_kernel(mine_ref, sibling_ref, first_ref, own_ref, gift_ref, sems):
    slots, half = own_ref.shape[:2]

    def start(s, carry):
        for i, (source, out) in enumerate([(mine_ref, own_ref), (sibling_ref, gift_ref)]):
            pltpu.make_async_copy(
                first_ref.at[source[s] >> 1, 0:half], out.at[s], sems.at[i]
            ).start()
        return carry

    lax.fori_loop(0, slots, start, 0, unroll=8)
    for i, out in enumerate([own_ref, gift_ref]):
        pltpu.make_async_copy(first_ref.at[0:slots, 0:half], out, sems.at[i]).wait()


def inverse_kernel(base_ref, order_ref, id_ref, place_ref):
    leaves, pts = id_ref.shape
    base = base_ref[0]
    row_id = lax.broadcasted_iota(jnp.int32, (pts, pts), 0)
    tile_id = lax.broadcasted_iota(jnp.int32, (leaves, pts), 0)
    position = lax.broadcasted_iota(jnp.int32, (leaves, pts), 1).astype(F32)

    def leaf(t, total):
        local = order_rows(order_ref, base, t)
        low = local & (pts - 1)
        high = local >> log2(pts)
        onehot = jnp.where(row_id == low, 1.0, 0.0).astype(BF16)
        here = jnp.where(tile_id == high, 1.0, 0.0)
        rows = jnp.concatenate([here * t.astype(F32), here * position], axis=0)
        return total + mm(rows.astype(BF16), onehot, NT)

    total = lax.fori_loop(0, leaves, leaf, jnp.zeros((2 * leaves, pts), F32), unroll=4)
    id_ref[...] = total[0:leaves].astype(jnp.int32)
    place_ref[...] = total[leaves:].astype(jnp.int32)


def near_kernel(
    me_ref, source_ref, count_ref, left_ref, tree_ref, right_ref, out_ref,
    x_all, target_c, source_c, block_ref, weight_ref, pair_ref,
):
    leaves, height, pts = tree_ref.shape
    vectors = out_ref.shape[1]
    reach = left_ref.shape[0]
    wide = leaves + 2 * reach
    window = 2 * reach + 1
    x_all[0:reach] = left_ref[:, 0:vectors]
    x_all[reach : reach + leaves] = tree_ref[:, 0:vectors]
    x_all[reach + leaves : wide] = right_ref[:, 0:vectors]
    out_ref[...] = jnp.zeros(out_ref.shape, F32)
    lanes = source_c.shape[2] // 3
    part = lax.broadcasted_iota(jnp.int32, (ROWS, 3 * lanes), 0)
    axis_of = lax.broadcasted_iota(jnp.int32, (ROWS, 3 * lanes), 1) // lanes
    chosen = (part == axis_of) | (part == axis_of + 3) | (part == axis_of + 6)
    spread = jnp.where(chosen, float(pts), 0.0).astype(BF16)

    def prepare(ref, count, offset, own):
        def step(l, carry):
            raw = ref[l, vectors:height]
            source_c[offset + l] = mm(raw, spread, TN)
            if own:
                raw = raw.astype(F32)
                target_c[l] = (raw[0:8] + raw[3:11] + raw[6:14]) * float(pts)
            return carry

        lax.fori_loop(0, count, step, 0, unroll=2)

    prepare(left_ref, reach, 0, False)
    prepare(tree_ref, leaves, reach, True)
    prepare(right_ref, reach, reach + leaves, False)

    def tally(t, carry):
        shift = t + me_ref[0] * leaves - reach
        near, far = 0, 0
        for n in range(source_ref.shape[1]):
            m = source_ref[t, n] - shift
            live = jnp.where(count_ref[t] > n, 1, 0)
            near = near + (jnp.where(m < 8, live, 0) << (4 * (m & 7)))
            far = far + jnp.where(m < 8, 0, live)
        weight_ref[t] = near
        weight_ref[t + leaves] = far
        return carry

    lax.fori_loop(0, leaves, tally, 0, unroll=2)

    def listing(s, count):
        for m in range(window):
            t = s - m
            inside = (t >= 0) & (t < leaves)
            at = jnp.where(inside, t, 0)
            word = weight_ref[at] >> (4 * m) if m < 8 else weight_ref[at + leaves]
            weight = jnp.where(inside, word & 15, 0)
            pair_ref[count] = s + 256 * at + 65536 * weight
            count = count + jnp.where(weight > 0, 1, 0)
        pair_ref[count] = s
        return count + (count & 1)

    count = lax.fori_loop(0, wide, listing, 0)
    for i in range(2 * GROUP):
        pair_ref[count + i] = reach
    soft = delta_square * float(pts) * float(pts)

    def group(g, carry):
        for i in range(GROUP):
            n = 2 * (g * GROUP + i)
            pair = (pair_ref[n], pair_ref[n + 1])
            s = pair[0] & 255
            both = [(p >> 8) & 255 for p in pair]
            for row in range(0, pts, CHUNK):
                rows = slice(row, row + CHUNK)
                source = [source_c[s, rows, axis * lanes : (axis + 1) * lanes] for axis in range(3)]
                for h, t in enumerate(both):
                    for c in range(pts // lanes):
                        at = slice(c * lanes, (c + 1) * lanes)
                        dx, dy, dz = [target_c[t, k : k + 1, at] - source[k] for k in range(3)]
                        squared = dx * dx + dy * dy + dz * dz + soft
                        block_ref[i, rows, h * pts + c * lanes : h * pts + (c + 1) * lanes] = (
                            lax.rsqrt(squared).astype(BF16)
                        )
            product = mm(x_all[s], block_ref[i])
            for h, t in enumerate(both):
                weight = (pair[h] >> 16).astype(F32)
                out_ref[t] += weight * product[:, h * pts : (h + 1) * pts]
        return carry

    lax.fori_loop(0, (count // 2 + GROUP - 1) // GROUP, group, 0)


def top_kernel(
    me_ref, source_ref, target_ref, live_ref, coupling_ref, own_ref, other_ref, out_ref, total
):
    slots, rank_k = coupling_ref.shape[:2]
    parents, vectors = out_ref.shape[:2]
    core = me_ref[0] & (parents - 1)
    total[...] = jnp.zeros(total.shape, F32)

    def step(s, carry):
        same = (source_ref[s] & (parents - 1)) == core
        got = jnp.where(same, own_ref[s].astype(F32), other_ref[s].astype(F32))
        full = jnp.concatenate([got, pltpu.roll(got, vectors, 1)], axis=0).astype(BF16)
        term = mm(coupling_ref[s], full).astype(BF16).astype(F32)
        weight = jnp.where(live_ref[s] > 0, 1.0, 0.0)
        total[target_ref[s]] += weight * term
        return carry

    lax.fori_loop(0, slots, step, 0, unroll=8)
    for q in range(parents):
        out_ref[q] = total[q].T[:vectors].astype(BF16)


def rank_kernel(
    leaf_bits, source_ref, live_ref, coupling_ref, half_ref, owner_ref, coupling_out, seen
):
    slots = source_ref.shape[0]
    coupling_out[...] = coupling_ref[...]

    def clear(i, carry):
        seen[i] = 0
        return carry

    lax.fori_loop(0, seen.shape[0], clear, 0, unroll=8)

    def rank(s, carry):
        owner = source_ref[s] >> leaf_bits
        half_ref[s] = jnp.where(live_ref[s] > 0, seen[owner], 2)
        owner_ref[s] = owner
        seen[owner] = 1
        return carry

    lax.fori_loop(0, slots, rank, 0, unroll=8)


def finish_kernel(
    target_ref, half_ref, owner_ref,
    got_ref, coupling_hbm, top_hbm, transfer_hbm, basis_hbm, near_ref, id_ref, place_ref,
    out_hbm,
    coupling_ref, top_ref, transfer_ref, basis_ref, onehot_ref,
    total, summed, out_ref, sems, out_sems, coupling_sems,
):
    pieces = coupling_sems.shape[0]
    part = coupling_ref.shape[0] // pieces
    spans = [slice(i * part, (i + 1) * part) for i in range(pieces)]
    coupling_copies = fetch(
        [(coupling_hbm.at[span], coupling_ref.at[span]) for span in spans], coupling_sems
    )
    copies = fetch(
        [
            (top_hbm, top_ref), (transfer_hbm, transfer_ref), (basis_hbm, basis_ref),
        ],
        sems,
    )
    slots, rank_k = coupling_ref.shape[:2]
    leaves, vectors, pts = near_ref.shape
    total[...] = jnp.zeros(total.shape, F32)
    side = lax.broadcasted_iota(jnp.int32, (rank_k, 2 * vectors), 1) // vectors
    row_id = lax.broadcasted_iota(jnp.int32, (pts, pts), 0)
    for q in range(leaves):
        hot = jnp.where(row_id == place_ref[q : q + 1], 1.0, 0.0)
        onehot_ref[:, q * pts : (q + 1) * pts] = hot.astype(BF16)

    def step(s, carry):
        term = mm(coupling_ref[s], got_ref[owner_ref[s]])
        term = term.astype(BF16).astype(F32)
        total[target_ref[s]] += jnp.where(side == half_ref[s], term, 0.0)
        return carry

    for span, copy in zip(spans, coupling_copies):
        copy.wait()
        lax.fori_loop(span.start, span.stop, step, 0, unroll=UNROLL)
    for copy in copies:
        copy.wait()
    for t in range(leaves):
        both = total[t]
        far = (both + pltpu.roll(both, vectors, 1)).T[:vectors]
        far = (far + mm(top_ref[t // 8], transfer_ref[t])).astype(BF16)
        value = mm(far, basis_ref[t]) + near_ref[t]
        summed[t * vectors : (t + 1) * vectors, :] = value.astype(BF16)

    out_copies = []
    for g in range(leaves // WIDE):
        leaf_id = jnp.concatenate([id_ref[g * WIDE + i : g * WIDE + i + 1] for i in range(WIDE)], axis=1)
        cols = slice(g * WIDE * pts, (g + 1) * WIDE * pts)
        spread = mm(summed[...], onehot_ref[:, cols])
        found = jnp.zeros((vectors, WIDE * pts), F32)
        for t in range(leaves):
            found = jnp.where(leaf_id == t, spread[t * vectors : (t + 1) * vectors], found)
        out_ref[:, cols] = found.astype(BF16)
        copy = pltpu.make_async_copy(out_ref.at[:, cols], out_hbm.at[:, cols], out_sems.at[g])
        copy.start()
        out_copies.append(copy)
    for copy in out_copies:
        copy.wait()


def smem():
    return pl.BlockSpec(memory_space=pltpu.SMEM)


def vmem():
    return pl.BlockSpec(memory_space=pltpu.VMEM)


def anywhere():
    return pl.BlockSpec(memory_space=pltpu.HBM)


def busy(microseconds):
    return pl.CostEstimate(
        flops=microseconds * 10**9, bytes_accessed=10**6, transcendentals=0
    )


def params(limit=SOME_VMEM):
    return pltpu.CompilerParams(vmem_limit_bytes=limit)


def shards(
    points, coords, leaf_order, leaf_basis, transfer, far_coupling, far_target, far_source,
    far_live, top_coupling, top_target, top_source, top_live, near_source, near_count,
):
    peers = lax.axis_size(AXIS)
    me = lax.axis_index(AXIS).astype(jnp.int32)
    vectors = points.shape[0]
    leaves, rank_k, pts = leaf_basis.shape
    parents = leaves // 8
    reach = leaves // 4
    height = vectors + ROWS
    slots = far_source.shape[0]
    me_s = me.reshape(1)
    base_s = me_s * (leaves * pts)
    order = leaf_order.reshape(2 * leaves, pts // 2)
    shape = jax.ShapeDtypeStruct

    tops = top_source.shape[0]
    half = rank_k // 2
    tree, head, tail, table, first = pl.pallas_call(
        tree_kernel,
        out_shape=[
            shape((leaves, height, pts), BF16),
            shape((reach, height, pts), BF16),
            shape((reach, height, pts), BF16),
            shape((2, leaves, rank_k, 2 * vectors), BF16),
            shape((peers, half + 8, 2 * vectors), BF16),
        ],
        in_specs=[smem()] + [anywhere()] * 5 + [vmem()] * 2,
        out_specs=[anywhere()] * 5,
        scratch_shapes=[
            pltpu.VMEM(points.shape, BF16),
            pltpu.VMEM(coords.shape, F32),
            pltpu.VMEM(order.shape, jnp.int32),
            pltpu.VMEM(leaf_basis.shape, BF16),
            pltpu.VMEM(transfer.shape, BF16),
            pltpu.VMEM((leaves * height, pts), BF16),
            pltpu.VMEM((ROWS, leaves * pts), F32),
            pltpu.VMEM((8, 2 * vectors), F32),
            pltpu.SemaphoreType.DMA((5,)),
            pltpu.VMEM((leaves, height, pts), BF16),
            pltpu.VMEM((2, leaves, rank_k, 2 * vectors), BF16),
            pltpu.VMEM((REPEAT, half + 8, 2 * vectors), BF16),
            pltpu.VMEM((parents, rank_k, 2 * vectors), F32),
            pltpu.SemaphoreType.DMA((4,)),
            pltpu.SemaphoreType.DMA((peers // REPEAT,)),
        ],
        compiler_params=params(MOST_VMEM),
        cost_estimate=busy(7),
        name="tree",
    )(
        base_s, points, coords, order, leaf_basis, transfer,
        far_source.reshape(1, slots), top_source.reshape(1, tops),
    )
    first = lax.all_to_all(first, AXIS, 0, 0, tiled=True)
    ends = peers - 1
    left = lax.ppermute(tail, AXIS, [(i, i + 1) for i in range(ends)])
    right = lax.ppermute(head, AXIS, [(i + 1, i) for i in range(ends)])
    ids, places = pl.pallas_call(
        inverse_kernel,
        out_shape=[shape((leaves, pts), jnp.int32)] * 2,
        in_specs=[smem(), vmem()],
        out_specs=[vmem(), vmem()],
        compiler_params=params(),
        cost_estimate=busy(3),
        name="inverse",
    )(base_s, order)
    halves, owners, coupling = pl.pallas_call(
        functools.partial(rank_kernel, log2(leaves)),
        out_shape=[shape((slots,), jnp.int32)] * 2 + [shape(far_coupling.shape, BF16)],
        in_specs=[smem()] * 2 + [vmem()],
        out_specs=[smem()] * 2 + [vmem()],
        scratch_shapes=[pltpu.SMEM((peers,), jnp.int32)],
        compiler_params=params(MOST_VMEM),
        cost_estimate=busy(3),
        name="rank",
    )(far_source, far_live, far_coupling)
    first, table, places, coupling, left, right = lax.optimization_barrier(
        (first, table, places, coupling, left, right)
    )
    send = pl.pallas_call(
        send_kernel,
        out_shape=shape((peers, rank_k, 2 * vectors), BF16),
        in_specs=[smem(), vmem(), anywhere()],
        out_specs=anywhere(),
        scratch_shapes=[
            pltpu.VMEM(table.shape, BF16),
            pltpu.VMEM((peers, rank_k, 2 * vectors), BF16),
            pltpu.VMEM((8, peers), jnp.int32),
            pltpu.SMEM((8, peers), jnp.int32),
            pltpu.SemaphoreType.DMA,
            pltpu.SemaphoreType.DMA,
            pltpu.SemaphoreType.DMA((4,)),
        ],
        compiler_params=params(SEND_VMEM),
        cost_estimate=busy(2),
        name="send",
    )(me_s, first, table)
    got = lax.all_to_all(send, AXIS, 0, 0, tiled=True)
    sibling = lax.dynamic_slice(first, (me ^ 1, half + 2, 0), (1, 2, tops))[0].astype(jnp.int32)
    sibling = sibling[0] * parents + sibling[1]
    block = shape((tops, half, 2 * vectors), BF16)
    own_blocks, gift = pl.pallas_call(
        gift_kernel,
        out_shape=[block, block],
        in_specs=[smem(), smem(), vmem()],
        out_specs=[vmem(), vmem()],
        scratch_shapes=[pltpu.SemaphoreType.DMA((2,))],
        compiler_params=params(),
        cost_estimate=busy(2),
        name="gift",
    )(top_source, sibling, first)
    other_blocks = lax.ppermute(gift, AXIS, [(i, i ^ 1) for i in range(peers)])
    near = pl.pallas_call(
        near_kernel,
        out_shape=shape((leaves, vectors, pts), F32),
        in_specs=[smem()] * 3 + [vmem()] * 3,
        out_specs=vmem(),
        scratch_shapes=[
            pltpu.VMEM((leaves + 2 * reach, vectors, pts), BF16),
            pltpu.VMEM((leaves, 8, pts), F32),
            pltpu.VMEM((leaves + 2 * reach, pts, 3 * 128), F32),
            pltpu.VMEM((GROUP, pts, 2 * pts), BF16),
            pltpu.SMEM((2 * leaves,), jnp.int32),
            pltpu.SMEM(((2 * reach + 2) * (leaves + 2 * reach) + 2 * GROUP + 2,), jnp.int32),
        ],
        compiler_params=params(),
        cost_estimate=busy(19),
        name="near",
    )(me_s, near_source, near_count, left, tree, right)
    top_far = pl.pallas_call(
        top_kernel,
        out_shape=shape((parents, vectors, rank_k), BF16),
        in_specs=[smem()] * 4 + [vmem()] * 3,
        out_specs=vmem(),
        scratch_shapes=[pltpu.VMEM((parents, rank_k, 2 * vectors), F32)],
        compiler_params=params(),
        cost_estimate=busy(2),
        name="top",
    )(me_s, top_source, top_target, top_live, top_coupling, own_blocks, other_blocks)
    got, near, top_far = lax.optimization_barrier((got, near, top_far))
    return pl.pallas_call(
        finish_kernel,
        out_shape=shape((vectors, leaves * pts), BF16),
        in_specs=[smem()] * 3 + [vmem()] + [anywhere()] * 4 + [vmem()] * 3,
        out_specs=anywhere(),
        scratch_shapes=[
            pltpu.VMEM(coupling.shape, BF16),
            pltpu.VMEM(top_far.shape, BF16),
            pltpu.VMEM(transfer.shape, BF16),
            pltpu.VMEM(leaf_basis.shape, BF16),
            pltpu.VMEM((pts, leaves * pts), BF16),
            pltpu.VMEM((leaves, rank_k, 2 * vectors), F32),
            pltpu.VMEM((leaves * vectors, pts), BF16),
            pltpu.VMEM((vectors, leaves * pts), BF16),
            pltpu.SemaphoreType.DMA((3,)),
            pltpu.SemaphoreType.DMA((leaves // WIDE,)),
            pltpu.SemaphoreType.DMA((4,)),
        ],
        compiler_params=params(LAST_VMEM),
        cost_estimate=busy(8),
        name="finish",
    )(
        far_target, halves, owners,
        got, coupling, top_far, transfer, leaf_basis, near, ids, places,
    )


def solution(mesh):
    placed = (
        P(None, AXIS), P(None, AXIS), P(AXIS), P(AXIS, None, None), P(AXIS, None, None),
        P(AXIS, None, None), P(AXIS), P(AXIS), P(AXIS), P(AXIS, None, None), P(AXIS), P(AXIS),
        P(AXIS), P(AXIS, None), P(AXIS),
    )
    return jax.shard_map(
        shards, mesh=mesh, in_specs=placed, out_specs=P(None, AXIS), check_vma=False
    )
```

profile of v0, /device:TPU:1, one launch (start us, length us, event | category | flops | bytes accessed | tf_op | source)
XLA Modules:
  0.0 88.0 jit_solution(15197518451053855673)
XLA Ops:
  0.0 7.2 %tree.1 = (bf16[16,80,256]{2,1,0:T(8,128)(2,1)}, bf16[4,80,256]{2,1,0:T(8,128)(2,1)}, bf16[4,80,256]{2,1,0:T(8,128)(2,1)}, bf16[2,16,64,128]{3,2,1,0:T(8,128)(2,1)}, bf16[128,40,128]{2,1,0:T(8,128)(2,1)}) custom-call(s32[1]{0:T(128)S(6)} %mul.11.base_ref, bf16[64,4096]{1,0:T(8,128)(2,1)} %points_hbm.1, f32[3,4096]{1,0:T(4,128)} %coords_hbm.1, ...), custom_call_target="tpu_custom_call" | custom-call | flops 7000000000 | bytes 1000000 | tf_op jit(solution)/shard_map/tree/pallas_call | solution.py:466
  7.3 0.0 copy-start.13
  7.3 11.5 %all-to-all-start = ((bf16[128,40,128]{2,1,0:T(8,128)(2,1)}), bf16[128,40,128]{2,1,0:T(8,128)(2,1)S(1)}, u32[]{:S(2)}, u32[]{:S(2)}) async-start(bf16[128,40,128]{2,1,0:T(8,128)(2,1)} %get-tuple-element.28), calls=%async_computation | async-start | bytes 2621440 | tf_op jit(solution)/shard_map/all_to_all | solution.py:501
  18.8 0.0 copy-start.1
  18.8 3.5 %collective-permute-start = (bf16[4,80,256]{2,1,0:T(8,128)(2,1)S(1)}, bf16[4,80,256]{2,1,0:T(8,128)(2,1)S(1)}, u32[]{:S(2)}, u32[]{:S(2)}) collective-permute-start(bf16[4,80,256]{2,1,0:T(8,128)(2,1)S(1)} %copy-done.15), channel_id=1, source_target_pairs={{0,1},{1,2},{2,3},{3,4},{4,5},{5,6},{6,7},{7,8},{8,9},{9,10},{10,1... | collective-permute-start | bytes 491528 | tf_op jit(solution)/shard_map/ppermute | solution.py:503
  22.4 1.9 %collective-permute-start.1 = (bf16[4,80,256]{2,1,0:T(8,128)(2,1)S(1)}, bf16[4,80,256]{2,1,0:T(8,128)(2,1)S(1)}, u32[]{:S(2)}, u32[]{:S(2)}) collective-permute-start(bf16[4,80,256]{2,1,0:T(8,128)(2,1)S(1)} %copy-done.14), channel_id=1, source_target_pairs={{1,0},{2,1},{3,2},{4,3},{5,4},{6,5},{7,6},{8,7},{9,8},{10,9},{11,1... | collective-permute-start | bytes 491528 | tf_op jit(solution)/shard_map/ppermute | solution.py:504
  24.3 3.7 %copy.16.coupling_ref = bf16[128,64,64]{2,1,0:T(8,128)(2,1)} copy(bf16[128,64,64]{0,2,1:T(8,128)(2,1)S(1)} %copy-done.13) | data formatting | bytes 2097152 | tf_op args[5]
  28.0 1.1 %inverse.1 = (s32[16,256]{1,0:T(8,128)S(1)}, s32[16,256]{1,0:T(8,128)S(1)}) custom-call(s32[1]{0:T(128)S(6)} %mul.11.base_ref, s32[32,128]{1,0:T(8,128)S(1)} %bitcast.7), custom_call_target="tpu_custom_call" | custom-call | flops 3000000000 | bytes 1000000 | tf_op jit(solution)/shard_map/inverse/pallas_call | solution.py:505
  29.2 0.6 copy-done.11
  29.7 0.6 copy-done.12
  30.3 4.0 %rank.1 = (s32[128]{0:T(128)}, s32[128]{0:T(128)}, bf16[128,64,64]{2,1,0:T(8,128)(2,1)}) custom-call(s32[128]{0:T(128)} %source_ref.3, s32[128]{0:T(128)} %live_ref.2, bf16[128,64,64]{2,1,0:T(8,128)(2,1)} %copy.16.coupling_ref), custom_call_target="tpu_custom_call" | custom-call | flops 3000000000 | bytes 1000000 | tf_op jit(solution)/shard_map/rank/pallas_call | solution.py:514
  34.4 2.1 %collective-permute-done.1.right_ref = bf16[4,80,256]{2,1,0:T(8,128)(2,1)S(1)} collective-permute-done((bf16[4,80,256]{2,1,0:T(8,128)(2,1)S(1)}, bf16[4,80,256]{2,1,0:T(8,128)(2,1)S(1)}, u32[]{:S(2)}, u32[]{:S(2)}) %collective-permute-start.1) | collective-permute-done | bytes 163872 | tf_op jit(solution)/shard_map/ppermute | solution.py:504
  36.5 4.2 %all-to-all-done.first_ref = bf16[128,40,128]{2,1,0:T(8,128)(2,1)S(1)} async-done(((bf16[128,40,128]{2,1,0:T(8,128)(2,1)}), bf16[128,40,128]{2,1,0:T(8,128)(2,1)S(1)}, u32[]{:S(2)}, u32[]{:S(2)}) %all-to-all-start) | async-done | bytes 1310752 | tf_op jit(solution)/shard_map/all_to_all | solution.py:501
  40.7 2.5 %send.1 = bf16[128,64,128]{2,1,0:T(8,128)(2,1)} custom-call(s32[1]{0:T(128)} %bitcast.me_ref, bf16[128,40,128]{2,1,0:T(8,128)(2,1)S(1)} %all-to-all-done.first_ref, bf16[2,16,64,128]{3,2,1,0:T(8,128)(2,1)S(1)} %copy-done.7), custom_call_target="tpu_custom_call" | custom-call | flops 2000000000 | bytes 1000000 | tf_op jit(solution)/shard_map/send/pallas_call | solution.py:527
  43.2 5.7 %all-to-all-start.1 = ((bf16[128,64,128]{2,1,0:T(8,128)(2,1)}), bf16[128,64,128]{2,1,0:T(8,128)(2,1)}, u32[]{:S(2)}, u32[]{:S(2)}) async-start(bf16[128,64,128]{2,1,0:T(8,128)(2,1)} %send.1), calls=%async_computation.1 | async-start | bytes 4194304 | tf_op jit(solution)/shard_map/all_to_all | solution.py:545
  48.9 0.0 copy-start.3
  49.0 1.6 %gift.1 = (bf16[32,32,128]{2,1,0:T(8,128)(2,1)S(1)}, bf16[32,32,128]{2,1,0:T(8,128)(2,1)S(1)}) custom-call(s32[32]{0:T(128)S(1)} %copy-done.4, s32[32]{0:T(128)S(1)} %add_bitcast_fusion.sibling_ref, bf16[128,40,128]{2,1,0:T(8,128)(2,1)S(1)} %all-to-all-done.first_ref), custom_call_target="tpu_custom_call" | custom-call | flops 2000000000 | bytes 1000000 | tf_op jit(solution)/shard_map/gift/pallas_call | solution.py:549
  50.5 1.4 %collective-permute-start.2 = (bf16[32,32,128]{2,1,0:T(8,128)(2,1)S(1)}, bf16[32,32,128]{2,1,0:T(8,128)(2,1)S(1)}, u32[]{:S(2)}, u32[]{:S(2)}) collective-permute-start(bf16[32,32,128]{2,1,0:T(8,128)(2,1)S(1)} %get-tuple-element.40), channel_id=1, source_target_pairs={{0,1},{1,0},{2,3},{3,2},{4,5},{5,4},{6,7},{7,6},{8,9},{9,8},{10,11... | collective-permute-start | bytes 786440 | tf_op jit(solution)/shard_map/ppermute | solution.py:559
  51.9 19.8 %near.1.near_ref = f32[16,64,256]{2,1,0:T(8,128)S(1)} custom-call(s32[1]{0:T(128)} %bitcast.me_ref, s32[16,12]{1,0:T(8,128)S(1)} %copy-done.2, s32[16]{0:T(128)S(1)} %copy-done.3, bf16[4,80,256]{2,1,0:T(8,128)(2,1)S(1)} %collective-permute-done.left_ref, bf16[16,80,256]{2,1,0:T(8,128)(2,1)S(1)} %copy-done.9, ...), custom_call_target="tpu_custom_call" | custom-call | flops 19000000512 | bytes 1000000 | tf_op jit(solution)/shard_map/near/pallas_call | solution.py:560
  71.7 0.9 %copy-done.8 = f32[16,64,256]{2,1,0:T(8,128)} copy-done((f32[16,64,256]{2,1,0:T(8,128)}, f32[16,64,256]{2,1,0:T(8,128)S(1)}, u32[]{:S(2)}) %copy-start.8) | copy-done | bytes 1048600
  72.7 1.7 %top.1.top_hbm = bf16[2,64,64]{2,1,0:T(8,128)(2,1)S(1)} custom-call(s32[1]{0:T(128)} %bitcast.me_ref, s32[32]{0:T(128)S(1)} %copy-done.4, s32[32]{0:T(128)S(1)} %copy-done.5, s32[32]{0:T(128)S(1)} %copy-done.6, bf16[32,64,64]{2,1,0:T(8,128)(2,1)S(1)} %copy-done, bf16[32,32,128]{2,1,0:T(8,128)(2,1)S(1)} %get-tuple-element.39.own_ref, ...), custom_call_target="tpu_custom_call" | custom-call | flops 2000000000 | bytes 1000000 | tf_op jit(solution)/shard_map/top/pallas_call | solution.py:577
  74.4 0.6 copy-done.10
  75.0 4.1 %all-to-all-done.1.got_ref = bf16[128,64,128]{2,1,0:T(8,128)(2,1)} async-done(((bf16[128,64,128]{2,1,0:T(8,128)(2,1)}), bf16[128,64,128]{2,1,0:T(8,128)(2,1)}, u32[]{:S(2)}, u32[]{:S(2)}) %all-to-all-start.1) | async-done | bytes 2097184 | tf_op jit(solution)/shard_map/all_to_all | solution.py:545
  79.1 8.7 %finish.1 = bf16[64,4096]{1,0:T(8,128)(2,1)} custom-call(s32[128]{0:T(128)} %target_ref.3, s32[128]{0:T(128)} %get-tuple-element.26.half_ref, s32[128]{0:T(128)} %get-tuple-element.27.owner_ref, bf16[128,64,128]{2,1,0:T(8,128)(2,1)} %all-to-all-done.1.got_ref, bf16[128,64,64]{2,1,0:T(8,128)(2,1)} %get-tuple-element.42.coupling_hbm, ...), custom_call_target="tpu_custom_call" | custom-call | flops 8000000000 | bytes 1000000 | tf_op jit(solution)/shard_map/finish/pallas_call | solution.py:588
  (29 shorter events, 0.1 us)
Async XLA Ops:
  7.3 11.6 %copy-start.15 = (bf16[4,80,256]{2,1,0:T(8,128)(2,1)S(1)}, bf16[4,80,256]{2,1,0:T(8,128)(2,1)}, u32[]{:S(2)}) copy-start(bf16[4,80,256]{2,1,0:T(8,128)(2,1)} %get-tuple-element.32) | copy-start | bytes 491524
  7.3 15.1 %copy-start.14 = (bf16[4,80,256]{2,1,0:T(8,128)(2,1)S(1)}, bf16[4,80,256]{2,1,0:T(8,128)(2,1)}, u32[]{:S(2)}) copy-start(bf16[4,80,256]{2,1,0:T(8,128)(2,1)} %get-tuple-element.33) | copy-start | bytes 491524
  7.3 17.0 %copy-start.13 = (bf16[128,64,64]{0,2,1:T(8,128)(2,1)S(1)}, bf16[128,64,64]{0,2,1:T(8,128)(2,1)}, u32[]{:S(2)}) copy-start(bf16[128,64,64]{0,2,1:T(8,128)(2,1)} %param.20) | copy-start | bytes 3145732
  7.3 33.4 %all-to-all-start = ((bf16[128,40,128]{2,1,0:T(8,128)(2,1)}), bf16[128,40,128]{2,1,0:T(8,128)(2,1)S(1)}, u32[]{:S(2)}, u32[]{:S(2)}) async-start(bf16[128,40,128]{2,1,0:T(8,128)(2,1)} %get-tuple-element.28), calls=%async_computation | async-start | bytes 2621440 | tf_op jit(solution)/shard_map/all_to_all | solution.py:501
  18.8 9.3 %copy-start.1 = (s32[4096]{0:T(1024)S(1)}, s32[4096]{0:T(1024)}, u32[]{:S(2)}) copy-start(s32[4096]{0:T(1024)} %param.17) | copy-start | bytes 49156
  18.8 15.5 %collective-permute-start = (bf16[4,80,256]{2,1,0:T(8,128)(2,1)S(1)}, bf16[4,80,256]{2,1,0:T(8,128)(2,1)S(1)}, u32[]{:S(2)}, u32[]{:S(2)}) collective-permute-start(bf16[4,80,256]{2,1,0:T(8,128)(2,1)S(1)} %copy-done.15), channel_id=1, source_target_pairs={{0,1},{1,2},{2,3},{3,4},{4,5},{5,6},{6,7},{7,8},{8,9},{9,10},{10,1... | collective-permute-start | bytes 491528 | tf_op jit(solution)/shard_map/ppermute | solution.py:503
  22.4 14.1 %collective-permute-start.1 = (bf16[4,80,256]{2,1,0:T(8,128)(2,1)S(1)}, bf16[4,80,256]{2,1,0:T(8,128)(2,1)S(1)}, u32[]{:S(2)}, u32[]{:S(2)}) collective-permute-start(bf16[4,80,256]{2,1,0:T(8,128)(2,1)S(1)} %copy-done.14), channel_id=1, source_target_pairs={{1,0},{2,1},{3,2},{4,3},{5,4},{6,5},{7,6},{8,7},{9,8},{10,9},{11,1... | collective-permute-start | bytes 491528 | tf_op jit(solution)/shard_map/ppermute | solution.py:504
  29.1 0.6 copy-start.11
  29.7 0.6 copy-start.12
  30.3 10.4 %copy-start.7 = (bf16[2,16,64,128]{3,2,1,0:T(8,128)(2,1)S(1)}, bf16[2,16,64,128]{3,2,1,0:T(8,128)(2,1)}, u32[]{:S(2)}) copy-start(bf16[2,16,64,128]{3,2,1,0:T(8,128)(2,1)} %get-tuple-element.35.table_hbm) | copy-start | bytes 1572868
  43.2 5.7 %copy-start.4 = (s32[32]{0:T(128)S(1)}, s32[32]{0:T(128)}, u32[]{:S(2)}) copy-start(s32[32]{0:T(128)} %source_ref.5) | copy-start | bytes 388
  43.2 35.9 %all-to-all-start.1 = ((bf16[128,64,128]{2,1,0:T(8,128)(2,1)}), bf16[128,64,128]{2,1,0:T(8,128)(2,1)}, u32[]{:S(2)}, u32[]{:S(2)}) async-start(bf16[128,64,128]{2,1,0:T(8,128)(2,1)} %send.1), calls=%async_computation.1 | async-start | bytes 4194304 | tf_op jit(solution)/shard_map/all_to_all | solution.py:545
  48.9 3.0 %copy-start.2 = (s32[16,12]{1,0:T(8,128)S(1)}, s32[16,12]{1,0:T(8,128)}, u32[]{:S(2)}) copy-start(s32[16,12]{1,0:T(8,128)} %source_ref.4) | copy-start | bytes 2308
  48.9 3.0 %copy-start.3 = (s32[16]{0:T(128)S(1)}, s32[16]{0:T(128)}, u32[]{:S(2)}) copy-start(s32[16]{0:T(128)} %count_ref.1) | copy-start | bytes 196
  49.0 3.0 %copy-start.9 = (bf16[16,80,256]{2,1,0:T(8,128)(2,1)S(1)}, bf16[16,80,256]{2,1,0:T(8,128)(2,1)}, u32[]{:S(2)}) copy-start(bf16[16,80,256]{2,1,0:T(8,128)(2,1)} %get-tuple-element.37.tree_ref) | copy-start | bytes 1966084
  50.5 22.1 %collective-permute-start.2 = (bf16[32,32,128]{2,1,0:T(8,128)(2,1)S(1)}, bf16[32,32,128]{2,1,0:T(8,128)(2,1)S(1)}, u32[]{:S(2)}, u32[]{:S(2)}) collective-permute-start(bf16[32,32,128]{2,1,0:T(8,128)(2,1)S(1)} %get-tuple-element.40), channel_id=1, source_target_pairs={{0,1},{1,0},{2,3},{3,2},{4,5},{5,4},{6,7},{7,6},{8,9},{9,8},{10,11... | collective-permute-start | bytes 786440 | tf_op jit(solution)/shard_map/ppermute | solution.py:559
  51.9 20.8 %copy-start = (bf16[32,64,64]{2,1,0:T(8,128)(2,1)S(1)}, bf16[32,64,64]{2,1,0:T(8,128)(2,1)}, u32[]{:S(2)}) copy-start(bf16[32,64,64]{2,1,0:T(8,128)(2,1)} %coupling_ref.2) | copy-start | bytes 786436
  51.9 20.8 %copy-start.5 = (s32[32]{0:T(128)S(1)}, s32[32]{0:T(128)}, u32[]{:S(2)}) copy-start(s32[32]{0:T(128)} %target_ref.2) | copy-start | bytes 388
  51.9 20.7 %copy-start.6 = (s32[32]{0:T(128)S(1)}, s32[32]{0:T(128)}, u32[]{:S(2)}) copy-start(s32[32]{0:T(128)} %live_ref.3) | copy-start | bytes 388
  71.7 1.0 %copy-start.8 = (f32[16,64,256]{2,1,0:T(8,128)}, f32[16,64,256]{2,1,0:T(8,128)S(1)}, u32[]{:S(2)}) copy-start(f32[16,64,256]{2,1,0:T(8,128)S(1)} %near.1.near_ref) | copy-start | bytes 3145732
  74.4 0.6 copy-start.10
where the time goes:
time: 88.4 us; the launch traced here: 88 us
  Pallas kernels  46.6 us (53%)
  starting transfers between devices  24 us (27%)
  waiting for transfers between devices  10.4 us (12%)
  local copies, waits for them, and re-layouts  6.53 us (7%)
    pallas_call x1, Pallas kernels, shards(): pl.pallas_call(near_kernel, out_shape=shape((leaves, vectors, pts), F32),...  19.8 us
    all_to_all x1, starting transfers between devices, shards(): first = lax.all_to_all(first, AXIS, 0, 0, tiled=True)  11.5 us
    pallas_call x1, Pallas kernels, shards(): pl.pallas_call(finish_kernel, out_shape=shape((vectors, leaves * pts), BF...  8.71 us
    pallas_call x1, Pallas kernels, shards(): pl.pallas_call(tree_kernel, out_shape=[shape((leaves, height, pts), BF16)...  7.25 us
    unnamed x33, local copies, waits for them, and re-layouts  6.53 us
    all_to_all x1, starting transfers between devices, shards(): got = lax.all_to_all(send, AXIS, 0, 0, tiled=True)  5.68 us
    all_to_all x1, waiting for transfers between devices, shards(): first = lax.all_to_all(first, AXIS, 0, 0, tiled=True)  4.22 us
    all_to_all x1, waiting for transfers between devices, shards(): got = lax.all_to_all(send, AXIS, 0, 0, tiled=True)  4.1 us
  transfers between devices with their start and end apart: 5, of which 3 were waited for; matrix products, arithmetic and copies ran while one was open for 4% of the time, Pallas kernels for 32%

commit v1 on v0

--- a/solution.py
+++ b/solution.py
@@ -14,7 +14,7 @@
 WIDE = 8
 CHUNK = 32
 REPEAT = 16
-UNROLL = 32
+UNROLL = 16
 MOST_VMEM = 60 * 1024 * 1024
 SOME_VMEM = 40 * 1024 * 1024
 SEND_VMEM = SOME_VMEM
@@ -56,7 +56,7 @@
     base_ref, points_hbm, coords_hbm, order_hbm, basis_hbm, transfer_hbm, far_ref, top_ref,
     tree_hbm, head_hbm, tail_hbm, table_hbm, first_hbm,
     points_ref, coords_ref, order_ref, basis_ref, transfer_ref, stacked, parts, extra, sems,
-    tree_ref, table_ref, first_ref, upward, out_sems, first_sem,
+    tree_ref, table_ref, first_ref, out_sems, first_sem,
 ):
     copies = fetch(
         [
@@ -108,14 +108,6 @@
             coeff = coeff.astype(BF16)
         return carry
 
-    lax.fori_loop(0, leaves // WIDE, gather, 0)
-    out_copies = fetch(
-        [
-            (table_ref, table_hbm), (tree_ref, tree_hbm), (tree_ref.at[0:reach], head_hbm),
-            (tree_ref.at[leaves - reach : leaves], tail_hbm),
-        ],
-        out_sems,
-    )
     half = rank_k // 2
     parents = leaves // 8
     extra[...] = jnp.zeros(extra.shape, F32)
@@ -124,29 +116,34 @@
     tops = top_ref.shape[1]
     extra[2:3, 0:tops] = (top_ref[...] >> log2(parents)).astype(F32)
     extra[3:4, 0:tops] = (top_ref[...] & (parents - 1)).astype(F32)
-    packed = []
+    repeat, couples = first_ref.shape[1], first_hbm.shape[0]
+    parent_copies = []
     for q in range(parents):
+        for g in range(8 * q // WIDE, max(8 * (q + 1) // WIDE, 8 * q // WIDE + 1)):
+            gather(g, 0)
         total = jnp.zeros((rank_k, 2 * vectors), F32)
         for c in range(8 * q, 8 * q + 8):
             total = total + mm(transfer_ref[c], table_ref[0, c] + table_ref[1, c])
         left = lax.broadcasted_iota(jnp.int32, (half, 2 * vectors), 1) < vectors
         block = jnp.where(left, total[:half], total[half:])
-        packed.append(jnp.concatenate([block, extra[...]], axis=0).astype(BF16))
-
-    part = first_ref.shape[0]
-    for i in range(part // parents):
-        for q in range(parents):
-            first_ref[parents * i + q] = packed[q]
-    peers = first_hbm.shape[0]
-    for i in range(peers // part):
-        pltpu.make_async_copy(
-            first_ref, first_hbm.at[i * part : (i + 1) * part], first_sem.at[i]
-        ).start()
-    for i in range(peers // part):
-        pltpu.make_async_copy(
-            first_ref, first_hbm.at[i * part : (i + 1) * part], first_sem.at[i]
-        ).wait()
-    for copy in out_copies:
+        block = jnp.concatenate([block, extra[...]], axis=0).astype(BF16)
+        for i in range(repeat):
+            first_ref[q, i] = block
+        parent_copies += fetch(
+            [
+                (first_ref.at[q], first_hbm.at[i * repeat : (i + 1) * repeat, q])
+                for i in range(couples // repeat)
+            ],
+            first_sem.at[q],
+        )
+    out_copies = fetch(
+        [
+            (table_ref, table_hbm), (tree_ref, tree_hbm), (tree_ref.at[0:reach], head_hbm),
+            (tree_ref.at[leaves - reach : leaves], tail_hbm),
+        ],
+        out_sems,
+    )
+    for copy in parent_copies + out_copies:
         copy.wait()
 
 
@@ -339,10 +336,9 @@
 
 
 def rank_kernel(
-    leaf_bits, source_ref, live_ref, coupling_ref, half_ref, owner_ref, coupling_out, seen
+    leaf_bits, source_ref, target_ref, live_ref, coupling_ref, word_ref, packed_ref, seen
 ):
     slots = source_ref.shape[0]
-    coupling_out[...] = coupling_ref[...]
 
     def clear(i, carry):
         seen[i] = 0
@@ -352,19 +348,26 @@
 
     def rank(s, carry):
         owner = source_ref[s] >> leaf_bits
-        half_ref[s] = jnp.where(live_ref[s] > 0, seen[owner], 2)
-        owner_ref[s] = owner
+        half = jnp.where(live_ref[s] > 0, seen[owner], 2)
+        word_ref[s] = owner + 256 * target_ref[s] + 65536 * half
         seen[owner] = 1
         return carry
 
     lax.fori_loop(0, slots, rank, 0, unroll=8)
 
+    def pack(s, carry):
+        pair = [coupling_ref[s], coupling_ref[s + slots // 2]]
+        packed_ref[s] = jnp.concatenate(pair, axis=1)
+        return carry
+
+    lax.fori_loop(0, slots // 2, pack, 0, unroll=8)
+
 
 def finish_kernel(
-    target_ref, half_ref, owner_ref,
-    got_ref, coupling_hbm, top_hbm, transfer_hbm, basis_hbm, near_ref, id_ref, place_ref,
+    word_ref,
+    got_ref, coupling_hbm, top_hbm, transfer_hbm, basis_hbm, near_hbm, id_ref, place_ref,
     out_hbm,
-    coupling_ref, top_ref, transfer_ref, basis_ref, onehot_ref,
+    coupling_ref, top_ref, transfer_ref, basis_ref, near_ref, onehot_ref,
     total, summed, out_ref, sems, out_sems, coupling_sems,
 ):
     pieces = coupling_sems.shape[0]
@@ -376,10 +379,11 @@
     copies = fetch(
         [
             (top_hbm, top_ref), (transfer_hbm, transfer_ref), (basis_hbm, basis_ref),
+            (near_hbm, near_ref),
         ],
         sems,
     )
-    slots, rank_k = coupling_ref.shape[:2]
+    rank_k = coupling_ref.shape[1]
     leaves, vectors, pts = near_ref.shape
     total[...] = jnp.zeros(total.shape, F32)
     side = lax.broadcasted_iota(jnp.int32, (rank_k, 2 * vectors), 1) // vectors
@@ -388,10 +392,13 @@
         hot = jnp.where(row_id == place_ref[q : q + 1], 1.0, 0.0)
         onehot_ref[:, q * pts : (q + 1) * pts] = hot.astype(BF16)
 
-    def step(s, carry):
-        term = mm(coupling_ref[s], got_ref[owner_ref[s]])
-        term = term.astype(BF16).astype(F32)
-        total[target_ref[s]] += jnp.where(side == half_ref[s], term, 0.0)
+    def step(i, carry):
+        both = coupling_ref[i]
+        for h in range(2):
+            word = word_ref[i + h * coupling_ref.shape[0]]
+            term = mm(both[:, h * rank_k : (h + 1) * rank_k], got_ref[word & 255])
+            term = term.astype(BF16).astype(F32)
+            total[(word >> 8) & 255] += jnp.where(side == (word >> 16), term, 0.0)
         return carry
 
     for span, copy in zip(spans, coupling_copies):
@@ -470,7 +477,7 @@
             shape((reach, height, pts), BF16),
             shape((reach, height, pts), BF16),
             shape((2, leaves, rank_k, 2 * vectors), BF16),
-            shape((peers, half + 8, 2 * vectors), BF16),
+            shape((peers // parents, parents, half + 8, 2 * vectors), BF16),
         ],
         in_specs=[smem()] + [anywhere()] * 5 + [vmem()] * 2,
         out_specs=[anywhere()] * 5,
@@ -486,10 +493,9 @@
             pltpu.SemaphoreType.DMA((5,)),
             pltpu.VMEM((leaves, height, pts), BF16),
             pltpu.VMEM((2, leaves, rank_k, 2 * vectors), BF16),
-            pltpu.VMEM((REPEAT, half + 8, 2 * vectors), BF16),
-            pltpu.VMEM((parents, rank_k, 2 * vectors), F32),
+            pltpu.VMEM((parents, REPEAT, half + 8, 2 * vectors), BF16),
             pltpu.SemaphoreType.DMA((4,)),
-            pltpu.SemaphoreType.DMA((peers // REPEAT,)),
+            pltpu.SemaphoreType.DMA((parents, peers // parents // REPEAT)),
         ],
         compiler_params=params(MOST_VMEM),
         cost_estimate=busy(7),
@@ -498,6 +504,7 @@
         base_s, points, coords, order, leaf_basis, transfer,
         far_source.reshape(1, slots), top_source.reshape(1, tops),
     )
+    first = first.reshape(peers, half + 8, 2 * vectors)
     first = lax.all_to_all(first, AXIS, 0, 0, tiled=True)
     ends = peers - 1
     left = lax.ppermute(tail, AXIS, [(i, i + 1) for i in range(ends)])
@@ -511,16 +518,19 @@
         cost_estimate=busy(3),
         name="inverse",
     )(base_s, order)
-    halves, owners, coupling = pl.pallas_call(
+    words, coupling = pl.pallas_call(
         functools.partial(rank_kernel, log2(leaves)),
-        out_shape=[shape((slots,), jnp.int32)] * 2 + [shape(far_coupling.shape, BF16)],
-        in_specs=[smem()] * 2 + [vmem()],
-        out_specs=[smem()] * 2 + [vmem()],
+        out_shape=[
+            shape((slots,), jnp.int32),
+            shape((slots // 2, rank_k, 2 * rank_k), BF16),
+        ],
+        in_specs=[smem()] * 3 + [vmem()],
+        out_specs=[smem(), vmem()],
         scratch_shapes=[pltpu.SMEM((peers,), jnp.int32)],
         compiler_params=params(MOST_VMEM),
         cost_estimate=busy(3),
         name="rank",
-    )(far_source, far_live, far_coupling)
+    )(far_source, far_target, far_live, far_coupling)
     first, table, places, coupling, left, right = lax.optimization_barrier(
         (first, table, places, coupling, left, right)
     )
@@ -588,18 +598,19 @@
     return pl.pallas_call(
         finish_kernel,
         out_shape=shape((vectors, leaves * pts), BF16),
-        in_specs=[smem()] * 3 + [vmem()] + [anywhere()] * 4 + [vmem()] * 3,
+        in_specs=[smem(), vmem()] + [anywhere()] * 5 + [vmem()] * 2,
         out_specs=anywhere(),
         scratch_shapes=[
             pltpu.VMEM(coupling.shape, BF16),
             pltpu.VMEM(top_far.shape, BF16),
             pltpu.VMEM(transfer.shape, BF16),
             pltpu.VMEM(leaf_basis.shape, BF16),
+            pltpu.VMEM(near.shape, F32),
             pltpu.VMEM((pts, leaves * pts), BF16),
             pltpu.VMEM((leaves, rank_k, 2 * vectors), F32),
             pltpu.VMEM((leaves * vectors, pts), BF16),
             pltpu.VMEM((vectors, leaves * pts), BF16),
-            pltpu.SemaphoreType.DMA((3,)),
+            pltpu.SemaphoreType.DMA((4,)),
             pltpu.SemaphoreType.DMA((leaves // WIDE,)),
             pltpu.SemaphoreType.DMA((4,)),
         ],
@@ -607,8 +618,7 @@
         cost_estimate=busy(8),
         name="finish",
     )(
-        far_target, halves, owners,
-        got, coupling, top_far, transfer, leaf_basis, near, ids, places,
+        words, got, coupling, top_far, transfer, leaf_basis, near, ids, places,
     )
 
 

time: 88.4 us -> 87.9 us (level)
  no operation moved by 1% of the time
where the time goes in v1:
time: 87.9 us; the launch traced here: 87.4 us
  Pallas kernels  46.3 us (53%)
  starting transfers between devices  24 us (27%)
  waiting for transfers between devices  10.1 us (11%)
  local copies, waits for them, and re-layouts  6.62 us (8%)
    pallas_call x1, Pallas kernels, shards(): pl.pallas_call(near_kernel, out_shape=shape((leaves, vectors, pts), F32),...  19.8 us
    all_to_all x1, starting transfers between devices, shards(): first = lax.all_to_all(first, AXIS, 0, 0, tiled=True)  11.5 us
    pallas_call x1, Pallas kernels, shards(): pl.pallas_call(finish_kernel, out_shape=shape((vectors, leaves * pts), BF...  8.44 us
    pallas_call x1, Pallas kernels, shards(): pl.pallas_call(tree_kernel, out_shape=[shape((leaves, height, pts), BF16)...  7.04 us
    unnamed x33, local copies, waits for them, and re-layouts  6.62 us
    all_to_all x1, starting transfers between devices, shards(): got = lax.all_to_all(send, AXIS, 0, 0, tiled=True)  5.68 us
    pallas_call x1, Pallas kernels, shards(): pl.pallas_call(functools.partial(rank_kernel, log2(leaves)), out_shape=[s...  4.24 us
    all_to_all x1, waiting for transfers between devices, shards(): first = lax.all_to_all(first, AXIS, 0, 0, tiled=True)  4.22 us
  transfers between devices with their start and end apart: 5, of which 3 were waited for; matrix products, arithmetic and copies ran while one was open for 4% of the time, Pallas kernels for 32%

profile of v1, /device:TPU:1, one launch (start us, length us, event | category | flops | bytes accessed | tf_op | source)
XLA Modules:
  0.0 87.4 jit_solution(6668276392358741487)
XLA Ops:
  0.0 7.0 %tree.1 = (bf16[16,80,256]{2,1,0:T(8,128)(2,1)}, bf16[4,80,256]{2,1,0:T(8,128)(2,1)}, bf16[4,80,256]{2,1,0:T(8,128)(2,1)}, bf16[2,16,64,128]{3,2,1,0:T(8,128)(2,1)}, bf16[64,2,40,128]{3,2,1,0:T(8,128)(2,1)}) custom-call(s32[1]{0:T(128)S(6)} %mul.11.base_ref, bf16[64,4096]{1,0:T(8,128)(2,1)} %points_hbm.1, f32[3,4096]{1,0:T(4,128)} %coords_hbm.1, ...), custom_call_target="tpu_custom_call" | custom-call | flops 7000000000 | bytes 1000000 | tf_op jit(solution)/shard_map/tree/pallas_call | solution.py:473
  7.1 0.0 copy-start.13
  7.1 11.5 %all-to-all-start = ((bf16[128,40,128]{2,1,0:T(8,128)(2,1)}), bf16[128,40,128]{2,1,0:T(8,128)(2,1)S(1)}, u32[]{:S(2)}, u32[]{:S(2)}) async-start(bf16[128,40,128]{2,1,0:T(8,128)(2,1)} %bitcast.10), calls=%async_computation | async-start | bytes 2621440 | tf_op jit(solution)/shard_map/all_to_all | solution.py:508
  18.6 3.5 %collective-permute-start = (bf16[4,80,256]{2,1,0:T(8,128)(2,1)S(1)}, bf16[4,80,256]{2,1,0:T(8,128)(2,1)S(1)}, u32[]{:S(2)}, u32[]{:S(2)}) collective-permute-start(bf16[4,80,256]{2,1,0:T(8,128)(2,1)S(1)} %copy-done.15), channel_id=1, source_target_pairs={{0,1},{1,2},{2,3},{3,4},{4,5},{5,6},{6,7},{7,8},{8,9},{9,10},{10,1... | collective-permute-start | bytes 491528 | tf_op jit(solution)/shard_map/ppermute | solution.py:510
  22.2 1.9 %collective-permute-start.1 = (bf16[4,80,256]{2,1,0:T(8,128)(2,1)S(1)}, bf16[4,80,256]{2,1,0:T(8,128)(2,1)S(1)}, u32[]{:S(2)}, u32[]{:S(2)}) collective-permute-start(bf16[4,80,256]{2,1,0:T(8,128)(2,1)S(1)} %copy-done.14), channel_id=1, source_target_pairs={{1,0},{2,1},{3,2},{4,3},{5,4},{6,5},{7,6},{8,7},{9,8},{10,9},{11,1... | collective-permute-start | bytes 491528 | tf_op jit(solution)/shard_map/ppermute | solution.py:511
  24.1 3.8 %copy.16.coupling_ref = bf16[128,64,64]{2,1,0:T(8,128)(2,1)} copy(bf16[128,64,64]{0,2,1:T(8,128)(2,1)S(1)} %copy-done.13) | data formatting | bytes 2097152 | tf_op args[5]
  27.9 1.1 %inverse.1 = (s32[16,256]{1,0:T(8,128)S(1)}, s32[16,256]{1,0:T(8,128)S(1)}) custom-call(s32[1]{0:T(128)S(6)} %mul.11.base_ref, s32[32,128]{1,0:T(8,128)S(1)} %bitcast.8), custom_call_target="tpu_custom_call" | custom-call | flops 3000000000 | bytes 1000000 | tf_op jit(solution)/shard_map/inverse/pallas_call | solution.py:512
  29.0 0.6 copy-done.11
  29.6 0.6 copy-done.12
  30.2 4.2 %rank.1 = (s32[128]{0:T(128)}, bf16[64,64,128]{2,1,0:T(8,128)(2,1)}) custom-call(s32[128]{0:T(128)} %source_ref.3, s32[128]{0:T(128)} %target_ref.2, s32[128]{0:T(128)} %live_ref.2, bf16[128,64,64]{2,1,0:T(8,128)(2,1)} %copy.16.coupling_ref), custom_call_target="tpu_custom_call" | custom-call | flops 3000000000 | bytes 1000000 | tf_op jit(solution)/shard_map/rank/pallas_call | solution.py:521
  34.5 1.8 %collective-permute-done.1.right_ref = bf16[4,80,256]{2,1,0:T(8,128)(2,1)S(1)} collective-permute-done((bf16[4,80,256]{2,1,0:T(8,128)(2,1)S(1)}, bf16[4,80,256]{2,1,0:T(8,128)(2,1)S(1)}, u32[]{:S(2)}, u32[]{:S(2)}) %collective-permute-start.1) | collective-permute-done | bytes 163872 | tf_op jit(solution)/shard_map/ppermute | solution.py:511
  36.3 4.2 %all-to-all-done.first_ref = bf16[128,40,128]{2,1,0:T(8,128)(2,1)S(1)} async-done(((bf16[128,40,128]{2,1,0:T(8,128)(2,1)}), bf16[128,40,128]{2,1,0:T(8,128)(2,1)S(1)}, u32[]{:S(2)}, u32[]{:S(2)}) %all-to-all-start) | async-done | bytes 1310752 | tf_op jit(solution)/shard_map/all_to_all | solution.py:508
  40.5 2.5 %send.1 = bf16[128,64,128]{2,1,0:T(8,128)(2,1)} custom-call(s32[1]{0:T(128)} %bitcast.me_ref, bf16[128,40,128]{2,1,0:T(8,128)(2,1)S(1)} %all-to-all-done.first_ref, bf16[2,16,64,128]{3,2,1,0:T(8,128)(2,1)S(1)} %copy-done.7), custom_call_target="tpu_custom_call" | custom-call | flops 2000000000 | bytes 1000000 | tf_op jit(solution)/shard_map/send/pallas_call | solution.py:537
  43.0 5.7 %all-to-all-start.1 = ((bf16[128,64,128]{2,1,0:T(8,128)(2,1)}), bf16[128,64,128]{2,1,0:T(8,128)(2,1)}, u32[]{:S(2)}, u32[]{:S(2)}) async-start(bf16[128,64,128]{2,1,0:T(8,128)(2,1)} %send.1), calls=%async_computation.1 | async-start | bytes 4194304 | tf_op jit(solution)/shard_map/all_to_all | solution.py:555
  48.7 0.0 copy-start.2
  48.7 1.6 %gift.1 = (bf16[32,32,128]{2,1,0:T(8,128)(2,1)S(1)}, bf16[32,32,128]{2,1,0:T(8,128)(2,1)S(1)}) custom-call(s32[32]{0:T(128)S(1)} %copy-done.4, s32[32]{0:T(128)S(1)} %add_bitcast_fusion.sibling_ref, bf16[128,40,128]{2,1,0:T(8,128)(2,1)S(1)} %all-to-all-done.first_ref), custom_call_target="tpu_custom_call" | custom-call | flops 2000000000 | bytes 1000000 | tf_op jit(solution)/shard_map/gift/pallas_call | solution.py:559
  50.3 1.4 %collective-permute-start.2 = (bf16[32,32,128]{2,1,0:T(8,128)(2,1)S(1)}, bf16[32,32,128]{2,1,0:T(8,128)(2,1)S(1)}, u32[]{:S(2)}, u32[]{:S(2)}) collective-permute-start(bf16[32,32,128]{2,1,0:T(8,128)(2,1)S(1)} %get-tuple-element.38), channel_id=1, source_target_pairs={{0,1},{1,0},{2,3},{3,2},{4,5},{5,4},{6,7},{7,6},{8,9},{9,8},{10,11... | collective-permute-start | bytes 786440 | tf_op jit(solution)/shard_map/ppermute | solution.py:569
  51.7 0.0 copy-start.5
  51.7 19.8 %near.1.near_hbm = f32[16,64,256]{2,1,0:T(8,128)S(1)} custom-call(s32[1]{0:T(128)} %bitcast.me_ref, s32[16,12]{1,0:T(8,128)S(1)} %copy-done.2, s32[16]{0:T(128)S(1)} %copy-done.3, bf16[4,80,256]{2,1,0:T(8,128)(2,1)S(1)} %collective-permute-done.left_ref, bf16[16,80,256]{2,1,0:T(8,128)(2,1)S(1)} %copy-done.9, ...), custom_call_target="tpu_custom_call" | custom-call | flops 19000000512 | bytes 1000000 | tf_op jit(solution)/shard_map/near/pallas_call | solution.py:570
  71.5 1.0 %copy-done.8 = f32[16,64,256]{2,1,0:T(8,128)} copy-done((f32[16,64,256]{2,1,0:T(8,128)}, f32[16,64,256]{2,1,0:T(8,128)S(1)}, u32[]{:S(2)}) %copy-start.8) | copy-done | bytes 1048600
  72.5 1.7 %top.1.top_hbm = bf16[2,64,64]{2,1,0:T(8,128)(2,1)S(1)} custom-call(s32[1]{0:T(128)} %bitcast.me_ref, s32[32]{0:T(128)S(1)} %copy-done.4, s32[32]{0:T(128)S(1)} %copy-done.5, s32[32]{0:T(128)S(1)} %copy-done.6, bf16[32,64,64]{2,1,0:T(8,128)(2,1)S(1)} %copy-done, bf16[32,32,128]{2,1,0:T(8,128)(2,1)S(1)} %get-tuple-element.37.own_ref, ...), custom_call_target="tpu_custom_call" | custom-call | flops 2000000000 | bytes 1000000 | tf_op jit(solution)/shard_map/top/pallas_call | solution.py:587
  74.2 0.6 copy-done.10
  74.7 4.1 %all-to-all-done.1.got_ref = bf16[128,64,128]{2,1,0:T(8,128)(2,1)} async-done(((bf16[128,64,128]{2,1,0:T(8,128)(2,1)}), bf16[128,64,128]{2,1,0:T(8,128)(2,1)}, u32[]{:S(2)}, u32[]{:S(2)}) %all-to-all-start.1) | async-done | bytes 2097184 | tf_op jit(solution)/shard_map/all_to_all | solution.py:555
  78.8 8.4 %finish.1 = bf16[64,4096]{1,0:T(8,128)(2,1)} custom-call(s32[128]{0:T(128)} %get-tuple-element.25.word_ref, bf16[128,64,128]{2,1,0:T(8,128)(2,1)} %all-to-all-done.1.got_ref, bf16[64,64,128]{2,1,0:T(8,128)(2,1)} %get-tuple-element.40.coupling_hbm, bf16[2,64,64]{2,1,0:T(8,128)(2,1)} %copy-done.10, bf16[16,64,64]{2,1,0:T(8,128)(2,1)} %transfer_hbm.3, ...), custom_call_target="tpu_custom_call" | custom-call | flops 8000000000 | bytes 1000000 | tf_op jit(solution)/shard_map/finish/pallas_call | solution.py:598
  (29 shorter events, 0.1 us)
Async XLA Ops:
  7.0 11.6 %copy-start.15 = (bf16[4,80,256]{2,1,0:T(8,128)(2,1)S(1)}, bf16[4,80,256]{2,1,0:T(8,128)(2,1)}, u32[]{:S(2)}) copy-start(bf16[4,80,256]{2,1,0:T(8,128)(2,1)} %get-tuple-element.30) | copy-start | bytes 491524
  7.1 15.1 %copy-start.14 = (bf16[4,80,256]{2,1,0:T(8,128)(2,1)S(1)}, bf16[4,80,256]{2,1,0:T(8,128)(2,1)}, u32[]{:S(2)}) copy-start(bf16[4,80,256]{2,1,0:T(8,128)(2,1)} %get-tuple-element.31) | copy-start | bytes 491524
  7.1 17.0 %copy-start.13 = (bf16[128,64,64]{0,2,1:T(8,128)(2,1)S(1)}, bf16[128,64,64]{0,2,1:T(8,128)(2,1)}, u32[]{:S(2)}) copy-start(bf16[128,64,64]{0,2,1:T(8,128)(2,1)} %param.20) | copy-start | bytes 3145732
  7.1 33.4 %all-to-all-start = ((bf16[128,40,128]{2,1,0:T(8,128)(2,1)}), bf16[128,40,128]{2,1,0:T(8,128)(2,1)S(1)}, u32[]{:S(2)}, u32[]{:S(2)}) async-start(bf16[128,40,128]{2,1,0:T(8,128)(2,1)} %bitcast.10), calls=%async_computation | async-start | bytes 2621440 | tf_op jit(solution)/shard_map/all_to_all | solution.py:508
  18.6 9.3 %copy-start.1 = (s32[4096]{0:T(1024)S(1)}, s32[4096]{0:T(1024)}, u32[]{:S(2)}) copy-start(s32[4096]{0:T(1024)} %param.17) | copy-start | bytes 49156
  18.6 15.8 %collective-permute-start = (bf16[4,80,256]{2,1,0:T(8,128)(2,1)S(1)}, bf16[4,80,256]{2,1,0:T(8,128)(2,1)S(1)}, u32[]{:S(2)}, u32[]{:S(2)}) collective-permute-start(bf16[4,80,256]{2,1,0:T(8,128)(2,1)S(1)} %copy-done.15), channel_id=1, source_target_pairs={{0,1},{1,2},{2,3},{3,4},{4,5},{5,6},{6,7},{7,8},{8,9},{9,10},{10,1... | collective-permute-start | bytes 491528 | tf_op jit(solution)/shard_map/ppermute | solution.py:510
  22.2 14.1 %collective-permute-start.1 = (bf16[4,80,256]{2,1,0:T(8,128)(2,1)S(1)}, bf16[4,80,256]{2,1,0:T(8,128)(2,1)S(1)}, u32[]{:S(2)}, u32[]{:S(2)}) collective-permute-start(bf16[4,80,256]{2,1,0:T(8,128)(2,1)S(1)} %copy-done.14), channel_id=1, source_target_pairs={{1,0},{2,1},{3,2},{4,3},{5,4},{6,5},{7,6},{8,7},{9,8},{10,9},{11,1... | collective-permute-start | bytes 491528 | tf_op jit(solution)/shard_map/ppermute | solution.py:511
  29.0 0.6 copy-start.11
  29.6 0.6 copy-start.12
  30.2 10.3 %copy-start.7 = (bf16[2,16,64,128]{3,2,1,0:T(8,128)(2,1)S(1)}, bf16[2,16,64,128]{3,2,1,0:T(8,128)(2,1)}, u32[]{:S(2)}) copy-start(bf16[2,16,64,128]{3,2,1,0:T(8,128)(2,1)} %get-tuple-element.33.table_hbm) | copy-start | bytes 1572868
  43.0 5.7 %copy-start.4 = (s32[32]{0:T(128)S(1)}, s32[32]{0:T(128)}, u32[]{:S(2)}) copy-start(s32[32]{0:T(128)} %source_ref.5) | copy-start | bytes 388
  43.0 35.9 %all-to-all-start.1 = ((bf16[128,64,128]{2,1,0:T(8,128)(2,1)}), bf16[128,64,128]{2,1,0:T(8,128)(2,1)}, u32[]{:S(2)}, u32[]{:S(2)}) async-start(bf16[128,64,128]{2,1,0:T(8,128)(2,1)} %send.1), calls=%async_computation.1 | async-start | bytes 4194304 | tf_op jit(solution)/shard_map/all_to_all | solution.py:555
  48.7 3.0 %copy-start.2 = (s32[16,12]{1,0:T(8,128)S(1)}, s32[16,12]{1,0:T(8,128)}, u32[]{:S(2)}) copy-start(s32[16,12]{1,0:T(8,128)} %source_ref.4) | copy-start | bytes 2308
  48.7 3.0 %copy-start.3 = (s32[16]{0:T(128)S(1)}, s32[16]{0:T(128)}, u32[]{:S(2)}) copy-start(s32[16]{0:T(128)} %count_ref.1) | copy-start | bytes 196
  48.7 3.0 %copy-start.9 = (bf16[16,80,256]{2,1,0:T(8,128)(2,1)S(1)}, bf16[16,80,256]{2,1,0:T(8,128)(2,1)}, u32[]{:S(2)}) copy-start(bf16[16,80,256]{2,1,0:T(8,128)(2,1)} %get-tuple-element.35.tree_ref) | copy-start | bytes 1966084
  50.3 22.1 %collective-permute-start.2 = (bf16[32,32,128]{2,1,0:T(8,128)(2,1)S(1)}, bf16[32,32,128]{2,1,0:T(8,128)(2,1)S(1)}, u32[]{:S(2)}, u32[]{:S(2)}) collective-permute-start(bf16[32,32,128]{2,1,0:T(8,128)(2,1)S(1)} %get-tuple-element.38), channel_id=1, source_target_pairs={{0,1},{1,0},{2,3},{3,2},{4,5},{5,4},{6,7},{7,6},{8,9},{9,8},{10,11... | collective-permute-start | bytes 786440 | tf_op jit(solution)/shard_map/ppermute | solution.py:569
  51.7 20.8 %copy-start = (bf16[32,64,64]{2,1,0:T(8,128)(2,1)S(1)}, bf16[32,64,64]{2,1,0:T(8,128)(2,1)}, u32[]{:S(2)}) copy-start(bf16[32,64,64]{2,1,0:T(8,128)(2,1)} %coupling_ref.2) | copy-start | bytes 786436
  51.7 20.8 %copy-start.5 = (s32[32]{0:T(128)S(1)}, s32[32]{0:T(128)}, u32[]{:S(2)}) copy-start(s32[32]{0:T(128)} %target_ref.3) | copy-start | bytes 388
  51.7 20.8 %copy-start.6 = (s32[32]{0:T(128)S(1)}, s32[32]{0:T(128)}, u32[]{:S(2)}) copy-start(s32[32]{0:T(128)} %live_ref.3) | copy-start | bytes 388
  71.5 1.0 %copy-start.8 = (f32[16,64,256]{2,1,0:T(8,128)}, f32[16,64,256]{2,1,0:T(8,128)S(1)}, u32[]{:S(2)}) copy-start(f32[16,64,256]{2,1,0:T(8,128)S(1)} %near.1.near_hbm) | copy-start | bytes 3145732
  74.1 0.6 copy-start.10

commit v2 on v1

--- a/solution.py
+++ b/solution.py
@@ -117,10 +117,21 @@
     extra[2:3, 0:tops] = (top_ref[...] >> log2(parents)).astype(F32)
     extra[3:4, 0:tops] = (top_ref[...] & (parents - 1)).astype(F32)
     repeat, couples = first_ref.shape[1], first_hbm.shape[0]
-    parent_copies = []
+    parent_copies, out_copies = [], []
     for q in range(parents):
         for g in range(8 * q // WIDE, max(8 * (q + 1) // WIDE, 8 * q // WIDE + 1)):
             gather(g, 0)
+        span = slice(8 * q, 8 * q + 8)
+        pairs = [
+            (table_ref.at[:, span], table_hbm.at[:, span]),
+            (tree_ref.at[span], tree_hbm.at[span]),
+        ]
+        if q == 0:
+            pairs.append((tree_ref.at[0:reach], head_hbm))
+        if q == parents - 1:
+            pairs.append((tree_ref.at[leaves - reach : leaves], tail_hbm))
+        if q < parents - 1:
+            out_copies += fetch(pairs, out_sems.at[q])
         total = jnp.zeros((rank_k, 2 * vectors), F32)
         for c in range(8 * q, 8 * q + 8):
             total = total + mm(transfer_ref[c], table_ref[0, c] + table_ref[1, c])
@@ -136,13 +147,8 @@
             ],
             first_sem.at[q],
         )
-    out_copies = fetch(
-        [
-            (table_ref, table_hbm), (tree_ref, tree_hbm), (tree_ref.at[0:reach], head_hbm),
-            (tree_ref.at[leaves - reach : leaves], tail_hbm),
-        ],
-        out_sems,
-    )
+        if q == parents - 1:
+            out_copies += fetch(pairs, out_sems.at[q])
     for copy in parent_copies + out_copies:
         copy.wait()
 
@@ -494,7 +500,7 @@
             pltpu.VMEM((leaves, height, pts), BF16),
             pltpu.VMEM((2, leaves, rank_k, 2 * vectors), BF16),
             pltpu.VMEM((parents, REPEAT, half + 8, 2 * vectors), BF16),
-            pltpu.SemaphoreType.DMA((4,)),
+            pltpu.SemaphoreType.DMA((parents, 4)),
             pltpu.SemaphoreType.DMA((parents, peers // parents // REPEAT)),
         ],
         compiler_params=params(MOST_VMEM),

time: 87.9 us -> 87.7 us (level)
  Pallas kernels: 46.3 us -> 45 us
  waiting for transfers between devices: 10.1 us -> 11.2 us
    pallas_call x1, Pallas kernels: 19.8 us -> 18.7 us  [shards(): pl.pallas_call(near_kernel, out_shape=shape((leaves, vectors, pts), F32),...]
    all_to_all x1, waiting for transfers between devices: 4.09 us -> 5.19 us  [shards(): got = lax.all_to_all(send, AXIS, 0, 0, tiled=True)]
  transfers between devices with their start and end apart: 5 -> 5, of which waited for: 3 -> 3; matrix products, arithmetic and copies ran while one was open for 4% -> 4% of each run, Pallas kernels for 32% -> 31%
where the time goes in v2:
time: 87.7 us; the launch traced here: 87.2 us
  Pallas kernels  45 us (51%)
  starting transfers between devices  24 us (27%)
  waiting for transfers between devices  11.2 us (13%)
  local copies, waits for them, and re-layouts  6.62 us (8%)
    pallas_call x1, Pallas kernels, shards(): pl.pallas_call(near_kernel, out_shape=shape((leaves, vectors, pts), F32),...  18.7 us
    all_to_all x1, starting transfers between devices, shards(): first = lax.all_to_all(first, AXIS, 0, 0, tiled=True)  11.5 us
    pallas_call x1, Pallas kernels, shards(): pl.pallas_call(finish_kernel, out_shape=shape((vectors, leaves * pts), BF...  8.44 us
    pallas_call x1, Pallas kernels, shards(): pl.pallas_call(tree_kernel, out_shape=[shape((leaves, height, pts), BF16)...  6.83 us
    unnamed x33, local copies, waits for them, and re-layouts  6.62 us
    all_to_all x1, starting transfers between devices, shards(): got = lax.all_to_all(send, AXIS, 0, 0, tiled=True)  5.68 us
    all_to_all x1, waiting for transfers between devices, shards(): got = lax.all_to_all(send, AXIS, 0, 0, tiled=True)  5.19 us
    pallas_call x1, Pallas kernels, shards(): pl.pallas_call(functools.partial(rank_kernel, log2(leaves)), out_shape=[s...  4.24 us
  transfers between devices with their start and end apart: 5, of which 3 were waited for; matrix products, arithmetic and copies ran while one was open for 4% of the time, Pallas kernels for 31%

profile of v2, /device:TPU:1, one launch (start us, length us, event | category | flops | bytes accessed | tf_op | source)
XLA Modules:
  0.0 87.2 jit_solution(406934904144931476)
XLA Ops:
  0.0 6.8 %tree.1 = (bf16[16,80,256]{2,1,0:T(8,128)(2,1)}, bf16[4,80,256]{2,1,0:T(8,128)(2,1)}, bf16[4,80,256]{2,1,0:T(8,128)(2,1)}, bf16[2,16,64,128]{3,2,1,0:T(8,128)(2,1)}, bf16[64,2,40,128]{3,2,1,0:T(8,128)(2,1)}) custom-call(s32[1]{0:T(128)S(6)} %mul.11.base_ref, bf16[64,4096]{1,0:T(8,128)(2,1)} %points_hbm.1, f32[3,4096]{1,0:T(4,128)} %coords_hbm.1, ...), custom_call_target="tpu_custom_call" | custom-call | flops 7000000000 | bytes 1000000 | tf_op jit(solution)/shard_map/tree/pallas_call | solution.py:479
  6.9 0.0 copy-start.13
  6.9 11.5 %all-to-all-start = ((bf16[128,40,128]{2,1,0:T(8,128)(2,1)}), bf16[128,40,128]{2,1,0:T(8,128)(2,1)S(1)}, u32[]{:S(2)}, u32[]{:S(2)}) async-start(bf16[128,40,128]{2,1,0:T(8,128)(2,1)} %bitcast.10), calls=%async_computation | async-start | bytes 2621440 | tf_op jit(solution)/shard_map/all_to_all | solution.py:514
  18.4 0.0 copy-start.1
  18.4 3.5 %collective-permute-start = (bf16[4,80,256]{2,1,0:T(8,128)(2,1)S(1)}, bf16[4,80,256]{2,1,0:T(8,128)(2,1)S(1)}, u32[]{:S(2)}, u32[]{:S(2)}) collective-permute-start(bf16[4,80,256]{2,1,0:T(8,128)(2,1)S(1)} %copy-done.15), channel_id=1, source_target_pairs={{0,1},{1,2},{2,3},{3,4},{4,5},{5,6},{6,7},{7,8},{8,9},{9,10},{10,1... | collective-permute-start | bytes 491528 | tf_op jit(solution)/shard_map/ppermute | solution.py:516
  22.0 1.9 %collective-permute-start.1 = (bf16[4,80,256]{2,1,0:T(8,128)(2,1)S(1)}, bf16[4,80,256]{2,1,0:T(8,128)(2,1)S(1)}, u32[]{:S(2)}, u32[]{:S(2)}) collective-permute-start(bf16[4,80,256]{2,1,0:T(8,128)(2,1)S(1)} %copy-done.14), channel_id=1, source_target_pairs={{1,0},{2,1},{3,2},{4,3},{5,4},{6,5},{7,6},{8,7},{9,8},{10,9},{11,1... | collective-permute-start | bytes 491528 | tf_op jit(solution)/shard_map/ppermute | solution.py:517
  23.9 3.8 %copy.16.coupling_ref = bf16[128,64,64]{2,1,0:T(8,128)(2,1)} copy(bf16[128,64,64]{0,2,1:T(8,128)(2,1)S(1)} %copy-done.13) | data formatting | bytes 2097152 | tf_op args[5]
  27.7 1.1 %inverse.1 = (s32[16,256]{1,0:T(8,128)S(1)}, s32[16,256]{1,0:T(8,128)S(1)}) custom-call(s32[1]{0:T(128)S(6)} %mul.11.base_ref, s32[32,128]{1,0:T(8,128)S(1)} %bitcast.8), custom_call_target="tpu_custom_call" | custom-call | flops 3000000000 | bytes 1000000 | tf_op jit(solution)/shard_map/inverse/pallas_call | solution.py:518
  28.8 0.6 copy-done.11
  29.4 0.6 copy-done.12
  30.0 4.2 %rank.1 = (s32[128]{0:T(128)}, bf16[64,64,128]{2,1,0:T(8,128)(2,1)}) custom-call(s32[128]{0:T(128)} %source_ref.3, s32[128]{0:T(128)} %target_ref.2, s32[128]{0:T(128)} %live_ref.2, bf16[128,64,64]{2,1,0:T(8,128)(2,1)} %copy.16.coupling_ref), custom_call_target="tpu_custom_call" | custom-call | flops 3000000000 | bytes 1000000 | tf_op jit(solution)/shard_map/rank/pallas_call | solution.py:527
  34.3 1.8 %collective-permute-done.1.right_ref = bf16[4,80,256]{2,1,0:T(8,128)(2,1)S(1)} collective-permute-done((bf16[4,80,256]{2,1,0:T(8,128)(2,1)S(1)}, bf16[4,80,256]{2,1,0:T(8,128)(2,1)S(1)}, u32[]{:S(2)}, u32[]{:S(2)}) %collective-permute-start.1) | collective-permute-done | bytes 163872 | tf_op jit(solution)/shard_map/ppermute | solution.py:517
  36.1 4.2 %all-to-all-done.first_ref = bf16[128,40,128]{2,1,0:T(8,128)(2,1)S(1)} async-done(((bf16[128,40,128]{2,1,0:T(8,128)(2,1)}), bf16[128,40,128]{2,1,0:T(8,128)(2,1)S(1)}, u32[]{:S(2)}, u32[]{:S(2)}) %all-to-all-start) | async-done | bytes 1310752 | tf_op jit(solution)/shard_map/all_to_all | solution.py:514
  40.3 2.5 %send.1 = bf16[128,64,128]{2,1,0:T(8,128)(2,1)} custom-call(s32[1]{0:T(128)} %bitcast.me_ref, bf16[128,40,128]{2,1,0:T(8,128)(2,1)S(1)} %all-to-all-done.first_ref, bf16[2,16,64,128]{3,2,1,0:T(8,128)(2,1)S(1)} %copy-done.7), custom_call_target="tpu_custom_call" | custom-call | flops 2000000000 | bytes 1000000 | tf_op jit(solution)/shard_map/send/pallas_call | solution.py:543
  42.8 0.0 copy-start.4
  42.8 5.7 %all-to-all-start.1 = ((bf16[128,64,128]{2,1,0:T(8,128)(2,1)}), bf16[128,64,128]{2,1,0:T(8,128)(2,1)}, u32[]{:S(2)}, u32[]{:S(2)}) async-start(bf16[128,64,128]{2,1,0:T(8,128)(2,1)} %send.1), calls=%async_computation.1 | async-start | bytes 4194304 | tf_op jit(solution)/shard_map/all_to_all | solution.py:561
  48.5 1.6 %gift.1 = (bf16[32,32,128]{2,1,0:T(8,128)(2,1)S(1)}, bf16[32,32,128]{2,1,0:T(8,128)(2,1)S(1)}) custom-call(s32[32]{0:T(128)S(1)} %copy-done.4, s32[32]{0:T(128)S(1)} %add_bitcast_fusion.sibling_ref, bf16[128,40,128]{2,1,0:T(8,128)(2,1)S(1)} %all-to-all-done.first_ref), custom_call_target="tpu_custom_call" | custom-call | flops 2000000000 | bytes 1000000 | tf_op jit(solution)/shard_map/gift/pallas_call | solution.py:565
  50.1 1.4 %collective-permute-start.2 = (bf16[32,32,128]{2,1,0:T(8,128)(2,1)S(1)}, bf16[32,32,128]{2,1,0:T(8,128)(2,1)S(1)}, u32[]{:S(2)}, u32[]{:S(2)}) collective-permute-start(bf16[32,32,128]{2,1,0:T(8,128)(2,1)S(1)} %get-tuple-element.38), channel_id=1, source_target_pairs={{0,1},{1,0},{2,3},{3,2},{4,5},{5,4},{6,7},{7,6},{8,9},{9,8},{10,11... | collective-permute-start | bytes 786440 | tf_op jit(solution)/shard_map/ppermute | solution.py:575
  51.5 18.7 %near.1.near_hbm = f32[16,64,256]{2,1,0:T(8,128)S(1)} custom-call(s32[1]{0:T(128)} %bitcast.me_ref, s32[16,12]{1,0:T(8,128)S(1)} %copy-done.2, s32[16]{0:T(128)S(1)} %copy-done.3, bf16[4,80,256]{2,1,0:T(8,128)(2,1)S(1)} %collective-permute-done.left_ref, bf16[16,80,256]{2,1,0:T(8,128)(2,1)S(1)} %copy-done.9, ...), custom_call_target="tpu_custom_call" | custom-call | flops 19000000512 | bytes 1000000 | tf_op jit(solution)/shard_map/near/pallas_call | solution.py:576
  70.2 1.0 %copy-done.8 = f32[16,64,256]{2,1,0:T(8,128)} copy-done((f32[16,64,256]{2,1,0:T(8,128)}, f32[16,64,256]{2,1,0:T(8,128)S(1)}, u32[]{:S(2)}) %copy-start.8) | copy-done | bytes 1048600
  71.1 1.7 %top.1.top_hbm = bf16[2,64,64]{2,1,0:T(8,128)(2,1)S(1)} custom-call(s32[1]{0:T(128)} %bitcast.me_ref, s32[32]{0:T(128)S(1)} %copy-done.4, s32[32]{0:T(128)S(1)} %copy-done.5, s32[32]{0:T(128)S(1)} %copy-done.6, bf16[32,64,64]{2,1,0:T(8,128)(2,1)S(1)} %copy-done, bf16[32,32,128]{2,1,0:T(8,128)(2,1)S(1)} %get-tuple-element.37.own_ref, ...), custom_call_target="tpu_custom_call" | custom-call | flops 2000000000 | bytes 1000000 | tf_op jit(solution)/shard_map/top/pallas_call | solution.py:593
  72.8 0.6 copy-done.10
  73.4 5.2 %all-to-all-done.1.got_ref = bf16[128,64,128]{2,1,0:T(8,128)(2,1)} async-done(((bf16[128,64,128]{2,1,0:T(8,128)(2,1)}), bf16[128,64,128]{2,1,0:T(8,128)(2,1)}, u32[]{:S(2)}, u32[]{:S(2)}) %all-to-all-start.1) | async-done | bytes 2097184 | tf_op jit(solution)/shard_map/all_to_all | solution.py:561
  78.6 8.4 %finish.1 = bf16[64,4096]{1,0:T(8,128)(2,1)} custom-call(s32[128]{0:T(128)} %get-tuple-element.25.word_ref, bf16[128,64,128]{2,1,0:T(8,128)(2,1)} %all-to-all-done.1.got_ref, bf16[64,64,128]{2,1,0:T(8,128)(2,1)} %get-tuple-element.40.coupling_hbm, bf16[2,64,64]{2,1,0:T(8,128)(2,1)} %copy-done.10, bf16[16,64,64]{2,1,0:T(8,128)(2,1)} %transfer_hbm.3, ...), custom_call_target="tpu_custom_call" | custom-call | flops 8000000000 | bytes 1000000 | tf_op jit(solution)/shard_map/finish/pallas_call | solution.py:604
  (29 shorter events, 0.1 us)
Async XLA Ops:
  6.8 11.6 %copy-start.15 = (bf16[4,80,256]{2,1,0:T(8,128)(2,1)S(1)}, bf16[4,80,256]{2,1,0:T(8,128)(2,1)}, u32[]{:S(2)}) copy-start(bf16[4,80,256]{2,1,0:T(8,128)(2,1)} %get-tuple-element.30) | copy-start | bytes 491524
  6.9 15.1 %copy-start.14 = (bf16[4,80,256]{2,1,0:T(8,128)(2,1)S(1)}, bf16[4,80,256]{2,1,0:T(8,128)(2,1)}, u32[]{:S(2)}) copy-start(bf16[4,80,256]{2,1,0:T(8,128)(2,1)} %get-tuple-element.31) | copy-start | bytes 491524
  6.9 17.0 %copy-start.13 = (bf16[128,64,64]{0,2,1:T(8,128)(2,1)S(1)}, bf16[128,64,64]{0,2,1:T(8,128)(2,1)}, u32[]{:S(2)}) copy-start(bf16[128,64,64]{0,2,1:T(8,128)(2,1)} %param.20) | copy-start | bytes 3145732
  6.9 33.4 %all-to-all-start = ((bf16[128,40,128]{2,1,0:T(8,128)(2,1)}), bf16[128,40,128]{2,1,0:T(8,128)(2,1)S(1)}, u32[]{:S(2)}, u32[]{:S(2)}) async-start(bf16[128,40,128]{2,1,0:T(8,128)(2,1)} %bitcast.10), calls=%async_computation | async-start | bytes 2621440 | tf_op jit(solution)/shard_map/all_to_all | solution.py:514
  18.4 9.3 %copy-start.1 = (s32[4096]{0:T(1024)S(1)}, s32[4096]{0:T(1024)}, u32[]{:S(2)}) copy-start(s32[4096]{0:T(1024)} %param.17) | copy-start | bytes 49156
  18.4 15.8 %collective-permute-start = (bf16[4,80,256]{2,1,0:T(8,128)(2,1)S(1)}, bf16[4,80,256]{2,1,0:T(8,128)(2,1)S(1)}, u32[]{:S(2)}, u32[]{:S(2)}) collective-permute-start(bf16[4,80,256]{2,1,0:T(8,128)(2,1)S(1)} %copy-done.15), channel_id=1, source_target_pairs={{0,1},{1,2},{2,3},{3,4},{4,5},{5,6},{6,7},{7,8},{8,9},{9,10},{10,1... | collective-permute-start | bytes 491528 | tf_op jit(solution)/shard_map/ppermute | solution.py:516
  22.0 14.1 %collective-permute-start.1 = (bf16[4,80,256]{2,1,0:T(8,128)(2,1)S(1)}, bf16[4,80,256]{2,1,0:T(8,128)(2,1)S(1)}, u32[]{:S(2)}, u32[]{:S(2)}) collective-permute-start(bf16[4,80,256]{2,1,0:T(8,128)(2,1)S(1)} %copy-done.14), channel_id=1, source_target_pairs={{1,0},{2,1},{3,2},{4,3},{5,4},{6,5},{7,6},{8,7},{9,8},{10,9},{11,1... | collective-permute-start | bytes 491528 | tf_op jit(solution)/shard_map/ppermute | solution.py:517
  28.8 0.6 copy-start.11
  29.4 0.6 copy-start.12
  30.0 10.3 %copy-start.7 = (bf16[2,16,64,128]{3,2,1,0:T(8,128)(2,1)S(1)}, bf16[2,16,64,128]{3,2,1,0:T(8,128)(2,1)}, u32[]{:S(2)}) copy-start(bf16[2,16,64,128]{3,2,1,0:T(8,128)(2,1)} %get-tuple-element.33.table_hbm) | copy-start | bytes 1572868
  42.8 5.7 %copy-start.4 = (s32[32]{0:T(128)S(1)}, s32[32]{0:T(128)}, u32[]{:S(2)}) copy-start(s32[32]{0:T(128)} %source_ref.5) | copy-start | bytes 388
  42.8 35.9 %all-to-all-start.1 = ((bf16[128,64,128]{2,1,0:T(8,128)(2,1)}), bf16[128,64,128]{2,1,0:T(8,128)(2,1)}, u32[]{:S(2)}, u32[]{:S(2)}) async-start(bf16[128,64,128]{2,1,0:T(8,128)(2,1)} %send.1), calls=%async_computation.1 | async-start | bytes 4194304 | tf_op jit(solution)/shard_map/all_to_all | solution.py:561
  48.5 3.0 %copy-start.2 = (s32[16,12]{1,0:T(8,128)S(1)}, s32[16,12]{1,0:T(8,128)}, u32[]{:S(2)}) copy-start(s32[16,12]{1,0:T(8,128)} %source_ref.4) | copy-start | bytes 2308
  48.5 3.0 %copy-start.3 = (s32[16]{0:T(128)S(1)}, s32[16]{0:T(128)}, u32[]{:S(2)}) copy-start(s32[16]{0:T(128)} %count_ref.1) | copy-start | bytes 196
  48.5 3.0 %copy-start.9 = (bf16[16,80,256]{2,1,0:T(8,128)(2,1)S(1)}, bf16[16,80,256]{2,1,0:T(8,128)(2,1)}, u32[]{:S(2)}) copy-start(bf16[16,80,256]{2,1,0:T(8,128)(2,1)} %get-tuple-element.35.tree_ref) | copy-start | bytes 1966084
  50.1 21.0 %collective-permute-start.2 = (bf16[32,32,128]{2,1,0:T(8,128)(2,1)S(1)}, bf16[32,32,128]{2,1,0:T(8,128)(2,1)S(1)}, u32[]{:S(2)}, u32[]{:S(2)}) collective-permute-start(bf16[32,32,128]{2,1,0:T(8,128)(2,1)S(1)} %get-tuple-element.38), channel_id=1, source_target_pairs={{0,1},{1,0},{2,3},{3,2},{4,5},{5,4},{6,7},{7,6},{8,9},{9,8},{10,11... | collective-permute-start | bytes 786440 | tf_op jit(solution)/shard_map/ppermute | solution.py:575
  51.4 19.7 %copy-start = (bf16[32,64,64]{2,1,0:T(8,128)(2,1)S(1)}, bf16[32,64,64]{2,1,0:T(8,128)(2,1)}, u32[]{:S(2)}) copy-start(bf16[32,64,64]{2,1,0:T(8,128)(2,1)} %coupling_ref.2) | copy-start | bytes 786436
  51.5 19.7 %copy-start.5 = (s32[32]{0:T(128)S(1)}, s32[32]{0:T(128)}, u32[]{:S(2)}) copy-start(s32[32]{0:T(128)} %target_ref.3) | copy-start | bytes 388
  51.5 19.7 %copy-start.6 = (s32[32]{0:T(128)S(1)}, s32[32]{0:T(128)}, u32[]{:S(2)}) copy-start(s32[32]{0:T(128)} %live_ref.3) | copy-start | bytes 388
  70.1 1.0 %copy-start.8 = (f32[16,64,256]{2,1,0:T(8,128)}, f32[16,64,256]{2,1,0:T(8,128)S(1)}, u32[]{:S(2)}) copy-start(f32[16,64,256]{2,1,0:T(8,128)S(1)} %near.1.near_hbm) | copy-start | bytes 3145732
  72.8 0.6 copy-start.10

commit v3 on v2

--- a/solution.py
+++ b/solution.py
@@ -15,6 +15,7 @@
 CHUNK = 32
 REPEAT = 16
 UNROLL = 16
+GOT = 4
 MOST_VMEM = 60 * 1024 * 1024
 SOME_VMEM = 40 * 1024 * 1024
 SEND_VMEM = SOME_VMEM
@@ -371,11 +372,14 @@
 
 def finish_kernel(
     word_ref,
-    got_ref, coupling_hbm, top_hbm, transfer_hbm, basis_hbm, near_hbm, id_ref, place_ref,
+    got_hbm, coupling_hbm, top_hbm, transfer_hbm, basis_hbm, near_hbm, id_ref, place_ref,
     out_hbm,
-    coupling_ref, top_ref, transfer_ref, basis_ref, near_ref, onehot_ref,
-    total, summed, out_ref, sems, out_sems, coupling_sems,
+    got_ref, coupling_ref, top_ref, transfer_ref, basis_ref, near_ref, onehot_ref,
+    total, summed, out_ref, sems, out_sems, coupling_sems, got_sems,
 ):
+    batch = got_ref.shape[0] // got_sems.shape[0]
+    shares = [slice(i * batch, (i + 1) * batch) for i in range(got_sems.shape[0])]
+    got_copies = fetch([(got_hbm.at[share], got_ref.at[share]) for share in shares], got_sems)
     pieces = coupling_sems.shape[0]
     part = coupling_ref.shape[0] // pieces
     spans = [slice(i * part, (i + 1) * part) for i in range(pieces)]
@@ -407,6 +411,8 @@
             total[(word >> 8) & 255] += jnp.where(side == (word >> 16), term, 0.0)
         return carry
 
+    for copy in got_copies:
+        copy.wait()
     for span, copy in zip(spans, coupling_copies):
         copy.wait()
         lax.fori_loop(span.start, span.stop, step, 0, unroll=UNROLL)
@@ -604,9 +610,10 @@
     return pl.pallas_call(
         finish_kernel,
         out_shape=shape((vectors, leaves * pts), BF16),
-        in_specs=[smem(), vmem()] + [anywhere()] * 5 + [vmem()] * 2,
+        in_specs=[smem()] + [anywhere()] * 6 + [vmem()] * 2,
         out_specs=anywhere(),
         scratch_shapes=[
+            pltpu.VMEM(got.shape, BF16),
             pltpu.VMEM(coupling.shape, BF16),
             pltpu.VMEM(top_far.shape, BF16),
             pltpu.VMEM(transfer.shape, BF16),
@@ -619,6 +626,7 @@
             pltpu.SemaphoreType.DMA((4,)),
             pltpu.SemaphoreType.DMA((leaves // WIDE,)),
             pltpu.SemaphoreType.DMA((4,)),
+            pltpu.SemaphoreType.DMA((GOT,)),
         ],
         compiler_params=params(LAST_VMEM),
         cost_estimate=busy(8),

time: 87.7 us -> 88 us (level)
  no operation moved by 1% of the time
where the time goes in v3:
time: 88 us; the launch traced here: 87.4 us
  Pallas kernels  45.2 us (51%)
  starting transfers between devices  24 us (27%)
  waiting for transfers between devices  11.2 us (13%)
  local copies, waits for them, and re-layouts  6.62 us (8%)
    pallas_call x1, Pallas kernels, shards(): pl.pallas_call(near_kernel, out_shape=shape((leaves, vectors, pts), F32),...  18.7 us
    all_to_all x1, starting transfers between devices, shards(): first = lax.all_to_all(first, AXIS, 0, 0, tiled=True)  11.5 us
    pallas_call x1, Pallas kernels, shards(): pl.pallas_call(finish_kernel, out_shape=shape((vectors, leaves * pts), BF...  8.65 us
    pallas_call x1, Pallas kernels, shards(): pl.pallas_call(tree_kernel, out_shape=[shape((leaves, height, pts), BF16)...  6.83 us
    unnamed x33, local copies, waits for them, and re-layouts  6.62 us
    all_to_all x1, starting transfers between devices, shards(): got = lax.all_to_all(send, AXIS, 0, 0, tiled=True)  5.68 us
    all_to_all x1, waiting for transfers between devices, shards(): got = lax.all_to_all(send, AXIS, 0, 0, tiled=True)  5.17 us
    pallas_call x1, Pallas kernels, shards(): pl.pallas_call(functools.partial(rank_kernel, log2(leaves)), out_shape=[s...  4.24 us
  transfers between devices with their start and end apart: 5, of which 3 were waited for; matrix products, arithmetic and copies ran while one was open for 4% of the time, Pallas kernels for 31%

profile of v3, /device:TPU:1, one launch (start us, length us, event | category | flops | bytes accessed | tf_op | source)
XLA Modules:
  0.0 87.4 jit_solution(945769964282085988)
XLA Ops:
  0.0 6.8 %tree.1 = (bf16[16,80,256]{2,1,0:T(8,128)(2,1)}, bf16[4,80,256]{2,1,0:T(8,128)(2,1)}, bf16[4,80,256]{2,1,0:T(8,128)(2,1)}, bf16[2,16,64,128]{3,2,1,0:T(8,128)(2,1)}, bf16[64,2,40,128]{3,2,1,0:T(8,128)(2,1)}) custom-call(s32[1]{0:T(128)S(6)} %mul.11.base_ref, bf16[64,4096]{1,0:T(8,128)(2,1)} %points_hbm.1, f32[3,4096]{1,0:T(4,128)} %coords_hbm.1, ...), custom_call_target="tpu_custom_call" | custom-call | flops 7000000000 | bytes 1000000 | tf_op jit(solution)/shard_map/tree/pallas_call | solution.py:485
  6.9 0.0 copy-start.13
  6.9 11.5 %all-to-all-start = ((bf16[128,40,128]{2,1,0:T(8,128)(2,1)}), bf16[128,40,128]{2,1,0:T(8,128)(2,1)S(1)}, u32[]{:S(2)}, u32[]{:S(2)}) async-start(bf16[128,40,128]{2,1,0:T(8,128)(2,1)} %bitcast.10), calls=%async_computation | async-start | bytes 2621440 | tf_op jit(solution)/shard_map/all_to_all | solution.py:520
  18.4 0.0 copy-start.1
  18.4 3.5 %collective-permute-start = (bf16[4,80,256]{2,1,0:T(8,128)(2,1)S(1)}, bf16[4,80,256]{2,1,0:T(8,128)(2,1)S(1)}, u32[]{:S(2)}, u32[]{:S(2)}) collective-permute-start(bf16[4,80,256]{2,1,0:T(8,128)(2,1)S(1)} %copy-done.15), channel_id=1, source_target_pairs={{0,1},{1,2},{2,3},{3,4},{4,5},{5,6},{6,7},{7,8},{8,9},{9,10},{10,1... | collective-permute-start | bytes 491528 | tf_op jit(solution)/shard_map/ppermute | solution.py:522
  22.0 1.9 %collective-permute-start.1 = (bf16[4,80,256]{2,1,0:T(8,128)(2,1)S(1)}, bf16[4,80,256]{2,1,0:T(8,128)(2,1)S(1)}, u32[]{:S(2)}, u32[]{:S(2)}) collective-permute-start(bf16[4,80,256]{2,1,0:T(8,128)(2,1)S(1)} %copy-done.14), channel_id=1, source_target_pairs={{1,0},{2,1},{3,2},{4,3},{5,4},{6,5},{7,6},{8,7},{9,8},{10,9},{11,1... | collective-permute-start | bytes 491528 | tf_op jit(solution)/shard_map/ppermute | solution.py:523
  23.9 3.8 %copy.16.coupling_ref = bf16[128,64,64]{2,1,0:T(8,128)(2,1)} copy(bf16[128,64,64]{0,2,1:T(8,128)(2,1)S(1)} %copy-done.13) | data formatting | bytes 2097152 | tf_op args[5]
  27.7 1.1 %inverse.1 = (s32[16,256]{1,0:T(8,128)S(1)}, s32[16,256]{1,0:T(8,128)S(1)}) custom-call(s32[1]{0:T(128)S(6)} %mul.11.base_ref, s32[32,128]{1,0:T(8,128)S(1)} %bitcast.8), custom_call_target="tpu_custom_call" | custom-call | flops 3000000000 | bytes 1000000 | tf_op jit(solution)/shard_map/inverse/pallas_call | solution.py:524
  28.8 0.6 copy-done.11
  29.4 0.6 copy-done.12
  30.0 4.2 %rank.1 = (s32[128]{0:T(128)}, bf16[64,64,128]{2,1,0:T(8,128)(2,1)}) custom-call(s32[128]{0:T(128)} %source_ref.3, s32[128]{0:T(128)} %target_ref.2, s32[128]{0:T(128)} %live_ref.2, bf16[128,64,64]{2,1,0:T(8,128)(2,1)} %copy.16.coupling_ref), custom_call_target="tpu_custom_call" | custom-call | flops 3000000000 | bytes 1000000 | tf_op jit(solution)/shard_map/rank/pallas_call | solution.py:533
  34.3 1.8 %collective-permute-done.1.right_ref = bf16[4,80,256]{2,1,0:T(8,128)(2,1)S(1)} collective-permute-done((bf16[4,80,256]{2,1,0:T(8,128)(2,1)S(1)}, bf16[4,80,256]{2,1,0:T(8,128)(2,1)S(1)}, u32[]{:S(2)}, u32[]{:S(2)}) %collective-permute-start.1) | collective-permute-done | bytes 163872 | tf_op jit(solution)/shard_map/ppermute | solution.py:523
  36.1 4.2 %all-to-all-done.first_ref = bf16[128,40,128]{2,1,0:T(8,128)(2,1)S(1)} async-done(((bf16[128,40,128]{2,1,0:T(8,128)(2,1)}), bf16[128,40,128]{2,1,0:T(8,128)(2,1)S(1)}, u32[]{:S(2)}, u32[]{:S(2)}) %all-to-all-start) | async-done | bytes 1310752 | tf_op jit(solution)/shard_map/all_to_all | solution.py:520
  40.3 2.5 %send.1 = bf16[128,64,128]{2,1,0:T(8,128)(2,1)} custom-call(s32[1]{0:T(128)} %bitcast.me_ref, bf16[128,40,128]{2,1,0:T(8,128)(2,1)S(1)} %all-to-all-done.first_ref, bf16[2,16,64,128]{3,2,1,0:T(8,128)(2,1)S(1)} %copy-done.7), custom_call_target="tpu_custom_call" | custom-call | flops 2000000000 | bytes 1000000 | tf_op jit(solution)/shard_map/send/pallas_call | solution.py:549
  42.8 5.7 %all-to-all-start.1 = ((bf16[128,64,128]{2,1,0:T(8,128)(2,1)}), bf16[128,64,128]{2,1,0:T(8,128)(2,1)}, u32[]{:S(2)}, u32[]{:S(2)}) async-start(bf16[128,64,128]{2,1,0:T(8,128)(2,1)} %send.1), calls=%async_computation.1 | async-start | bytes 4194304 | tf_op jit(solution)/shard_map/all_to_all | solution.py:567
  48.5 0.0 copy-start.2
  48.5 1.6 %gift.1 = (bf16[32,32,128]{2,1,0:T(8,128)(2,1)S(1)}, bf16[32,32,128]{2,1,0:T(8,128)(2,1)S(1)}) custom-call(s32[32]{0:T(128)S(1)} %copy-done.4, s32[32]{0:T(128)S(1)} %add_bitcast_fusion.sibling_ref, bf16[128,40,128]{2,1,0:T(8,128)(2,1)S(1)} %all-to-all-done.first_ref), custom_call_target="tpu_custom_call" | custom-call | flops 2000000000 | bytes 1000000 | tf_op jit(solution)/shard_map/gift/pallas_call | solution.py:571
  50.1 1.4 %collective-permute-start.2 = (bf16[32,32,128]{2,1,0:T(8,128)(2,1)S(1)}, bf16[32,32,128]{2,1,0:T(8,128)(2,1)S(1)}, u32[]{:S(2)}, u32[]{:S(2)}) collective-permute-start(bf16[32,32,128]{2,1,0:T(8,128)(2,1)S(1)} %get-tuple-element.38), channel_id=1, source_target_pairs={{0,1},{1,0},{2,3},{3,2},{4,5},{5,4},{6,7},{7,6},{8,9},{9,8},{10,11... | collective-permute-start | bytes 786440 | tf_op jit(solution)/shard_map/ppermute | solution.py:581
  51.5 18.7 %near.1.near_hbm = f32[16,64,256]{2,1,0:T(8,128)S(1)} custom-call(s32[1]{0:T(128)} %bitcast.me_ref, s32[16,12]{1,0:T(8,128)S(1)} %copy-done.2, s32[16]{0:T(128)S(1)} %copy-done.3, bf16[4,80,256]{2,1,0:T(8,128)(2,1)S(1)} %collective-permute-done.left_ref, bf16[16,80,256]{2,1,0:T(8,128)(2,1)S(1)} %copy-done.9, ...), custom_call_target="tpu_custom_call" | custom-call | flops 19000000512 | bytes 1000000 | tf_op jit(solution)/shard_map/near/pallas_call | solution.py:582
  70.2 1.0 %copy-done.8 = f32[16,64,256]{2,1,0:T(8,128)} copy-done((f32[16,64,256]{2,1,0:T(8,128)}, f32[16,64,256]{2,1,0:T(8,128)S(1)}, u32[]{:S(2)}) %copy-start.8) | copy-done | bytes 1048600
  71.1 1.7 %top.1.top_hbm = bf16[2,64,64]{2,1,0:T(8,128)(2,1)S(1)} custom-call(s32[1]{0:T(128)} %bitcast.me_ref, s32[32]{0:T(128)S(1)} %copy-done.4, s32[32]{0:T(128)S(1)} %copy-done.5, s32[32]{0:T(128)S(1)} %copy-done.6, bf16[32,64,64]{2,1,0:T(8,128)(2,1)S(1)} %copy-done, bf16[32,32,128]{2,1,0:T(8,128)(2,1)S(1)} %get-tuple-element.37.own_ref, ...), custom_call_target="tpu_custom_call" | custom-call | flops 2000000000 | bytes 1000000 | tf_op jit(solution)/shard_map/top/pallas_call | solution.py:599
  72.9 0.6 copy-done.10
  73.5 5.2 %all-to-all-done.1.got_hbm = bf16[128,64,128]{2,1,0:T(8,128)(2,1)} async-done(((bf16[128,64,128]{2,1,0:T(8,128)(2,1)}), bf16[128,64,128]{2,1,0:T(8,128)(2,1)}, u32[]{:S(2)}, u32[]{:S(2)}) %all-to-all-start.1) | async-done | bytes 2097184 | tf_op jit(solution)/shard_map/all_to_all | solution.py:567
  78.6 8.6 %finish.1 = bf16[64,4096]{1,0:T(8,128)(2,1)} custom-call(s32[128]{0:T(128)} %get-tuple-element.25.word_ref, bf16[128,64,128]{2,1,0:T(8,128)(2,1)} %all-to-all-done.1.got_hbm, bf16[64,64,128]{2,1,0:T(8,128)(2,1)} %get-tuple-element.40.coupling_hbm, bf16[2,64,64]{2,1,0:T(8,128)(2,1)} %copy-done.10, bf16[16,64,64]{2,1,0:T(8,128)(2,1)} %transfer_hbm.3, ...), custom_call_target="tpu_custom_call" | custom-call | flops 8000000000 | bytes 1000000 | tf_op jit(solution)/shard_map/finish/pallas_call | solution.py:610
  (29 shorter events, 0.1 us)
Async XLA Ops:
  6.8 11.6 %copy-start.15 = (bf16[4,80,256]{2,1,0:T(8,128)(2,1)S(1)}, bf16[4,80,256]{2,1,0:T(8,128)(2,1)}, u32[]{:S(2)}) copy-start(bf16[4,80,256]{2,1,0:T(8,128)(2,1)} %get-tuple-element.30) | copy-start | bytes 491524
  6.9 15.1 %copy-start.14 = (bf16[4,80,256]{2,1,0:T(8,128)(2,1)S(1)}, bf16[4,80,256]{2,1,0:T(8,128)(2,1)}, u32[]{:S(2)}) copy-start(bf16[4,80,256]{2,1,0:T(8,128)(2,1)} %get-tuple-element.31) | copy-start | bytes 491524
  6.9 17.0 %copy-start.13 = (bf16[128,64,64]{0,2,1:T(8,128)(2,1)S(1)}, bf16[128,64,64]{0,2,1:T(8,128)(2,1)}, u32[]{:S(2)}) copy-start(bf16[128,64,64]{0,2,1:T(8,128)(2,1)} %param.20) | copy-start | bytes 3145732
  6.9 33.4 %all-to-all-start = ((bf16[128,40,128]{2,1,0:T(8,128)(2,1)}), bf16[128,40,128]{2,1,0:T(8,128)(2,1)S(1)}, u32[]{:S(2)}, u32[]{:S(2)}) async-start(bf16[128,40,128]{2,1,0:T(8,128)(2,1)} %bitcast.10), calls=%async_computation | async-start | bytes 2621440 | tf_op jit(solution)/shard_map/all_to_all | solution.py:520
  18.4 9.3 %copy-start.1 = (s32[4096]{0:T(1024)S(1)}, s32[4096]{0:T(1024)}, u32[]{:S(2)}) copy-start(s32[4096]{0:T(1024)} %param.17) | copy-start | bytes 49156
  18.4 15.8 %collective-permute-start = (bf16[4,80,256]{2,1,0:T(8,128)(2,1)S(1)}, bf16[4,80,256]{2,1,0:T(8,128)(2,1)S(1)}, u32[]{:S(2)}, u32[]{:S(2)}) collective-permute-start(bf16[4,80,256]{2,1,0:T(8,128)(2,1)S(1)} %copy-done.15), channel_id=1, source_target_pairs={{0,1},{1,2},{2,3},{3,4},{4,5},{5,6},{6,7},{7,8},{8,9},{9,10},{10,1... | collective-permute-start | bytes 491528 | tf_op jit(solution)/shard_map/ppermute | solution.py:522
  22.0 14.1 %collective-permute-start.1 = (bf16[4,80,256]{2,1,0:T(8,128)(2,1)S(1)}, bf16[4,80,256]{2,1,0:T(8,128)(2,1)S(1)}, u32[]{:S(2)}, u32[]{:S(2)}) collective-permute-start(bf16[4,80,256]{2,1,0:T(8,128)(2,1)S(1)} %copy-done.14), channel_id=1, source_target_pairs={{1,0},{2,1},{3,2},{4,3},{5,4},{6,5},{7,6},{8,7},{9,8},{10,9},{11,1... | collective-permute-start | bytes 491528 | tf_op jit(solution)/shard_map/ppermute | solution.py:523
  28.8 0.6 copy-start.11
  29.4 0.6 copy-start.12
  30.0 10.3 %copy-start.7 = (bf16[2,16,64,128]{3,2,1,0:T(8,128)(2,1)S(1)}, bf16[2,16,64,128]{3,2,1,0:T(8,128)(2,1)}, u32[]{:S(2)}) copy-start(bf16[2,16,64,128]{3,2,1,0:T(8,128)(2,1)} %get-tuple-element.33.table_hbm) | copy-start | bytes 1572868
  42.8 5.7 %copy-start.4 = (s32[32]{0:T(128)S(1)}, s32[32]{0:T(128)}, u32[]{:S(2)}) copy-start(s32[32]{0:T(128)} %source_ref.5) | copy-start | bytes 388
  42.8 35.9 %all-to-all-start.1 = ((bf16[128,64,128]{2,1,0:T(8,128)(2,1)}), bf16[128,64,128]{2,1,0:T(8,128)(2,1)}, u32[]{:S(2)}, u32[]{:S(2)}) async-start(bf16[128,64,128]{2,1,0:T(8,128)(2,1)} %send.1), calls=%async_computation.1 | async-start | bytes 4194304 | tf_op jit(solution)/shard_map/all_to_all | solution.py:567
  48.5 3.0 %copy-start.2 = (s32[16,12]{1,0:T(8,128)S(1)}, s32[16,12]{1,0:T(8,128)}, u32[]{:S(2)}) copy-start(s32[16,12]{1,0:T(8,128)} %source_ref.4) | copy-start | bytes 2308
  48.5 3.0 %copy-start.3 = (s32[16]{0:T(128)S(1)}, s32[16]{0:T(128)}, u32[]{:S(2)}) copy-start(s32[16]{0:T(128)} %count_ref.1) | copy-start | bytes 196
  48.5 3.0 %copy-start.9 = (bf16[16,80,256]{2,1,0:T(8,128)(2,1)S(1)}, bf16[16,80,256]{2,1,0:T(8,128)(2,1)}, u32[]{:S(2)}) copy-start(bf16[16,80,256]{2,1,0:T(8,128)(2,1)} %get-tuple-element.35.tree_ref) | copy-start | bytes 1966084
  50.1 21.0 %collective-permute-start.2 = (bf16[32,32,128]{2,1,0:T(8,128)(2,1)S(1)}, bf16[32,32,128]{2,1,0:T(8,128)(2,1)S(1)}, u32[]{:S(2)}, u32[]{:S(2)}) collective-permute-start(bf16[32,32,128]{2,1,0:T(8,128)(2,1)S(1)} %get-tuple-element.38), channel_id=1, source_target_pairs={{0,1},{1,0},{2,3},{3,2},{4,5},{5,4},{6,7},{7,6},{8,9},{9,8},{10,11... | collective-permute-start | bytes 786440 | tf_op jit(solution)/shard_map/ppermute | solution.py:581
  51.4 19.7 %copy-start = (bf16[32,64,64]{2,1,0:T(8,128)(2,1)S(1)}, bf16[32,64,64]{2,1,0:T(8,128)(2,1)}, u32[]{:S(2)}) copy-start(bf16[32,64,64]{2,1,0:T(8,128)(2,1)} %coupling_ref.2) | copy-start | bytes 786436
  51.5 19.7 %copy-start.5 = (s32[32]{0:T(128)S(1)}, s32[32]{0:T(128)}, u32[]{:S(2)}) copy-start(s32[32]{0:T(128)} %target_ref.3) | copy-start | bytes 388
  51.5 19.7 %copy-start.6 = (s32[32]{0:T(128)S(1)}, s32[32]{0:T(128)}, u32[]{:S(2)}) copy-start(s32[32]{0:T(128)} %live_ref.3) | copy-start | bytes 388
  70.1 1.0 %copy-start.8 = (f32[16,64,256]{2,1,0:T(8,128)}, f32[16,64,256]{2,1,0:T(8,128)S(1)}, u32[]{:S(2)}) copy-start(f32[16,64,256]{2,1,0:T(8,128)S(1)} %near.1.near_hbm) | copy-start | bytes 3145732
  72.9 0.6 copy-start.10
